TPU v7x, 256 devices: a whole 4x4x8 slice. The times are simulated.
256 devices in a mesh: sect: 8 (over z_lo, y), tile: 32 (over z_hi, x, core).
Axes of the slice: x: 4, y: 4, z: 8 (z_hi: 4, z_lo: 2; z = z_hi * 2 + z_lo), core: 2. Of those that a mesh axis runs over, the one named last changes fastest.
Arguments:
- irrep_counts: int32 [2], replicated, may hold values from 64 to 128
- chol_left: bfloat16 [896, 256, 128], P('sect', 'tile'), may hold values from -0.15625 to 0.15625
- chol_right: bfloat16 [896, 128, 256], P(None, 'sect'), may hold values from -0.15625 to 0.15625
- lam: bfloat16 [512, 256, 256], P('sect', 'tile'), may hold values from -6 to 6
Outputs:
- ladder: bfloat16 [512, 128, 128], P('tile', None, 'sect')
Inputs may be any that keep to these rules, and one draw needn't show every extreme that they name: Orbital p of irrep k is live when p < irrep_counts[k].
All inputs are finite; a program needn't handle non-finite values.
Results may differ from a plain program's by a relative error of at most 0.0049.
Values may be sent and summed in bfloat16 or wider, within the bound.
A program may use at most 64 MiB of HBM per device.

v0:
```python
import jax
import jax.numpy as jnp
from jax import lax
from jax.sharding import PartitionSpec as P


def per_device(irrep_counts, chol_left, chol_right, lam):
    left_all = lax.all_gather(chol_left, "sect", axis=0, tiled=True)
    lam_all = lax.all_gather(lam, "sect", axis=0, tiled=True)
    aux_count, width_inner, virt_count = left_all.shape
    width_outer = chol_right.shape[1]
    positions = jnp.arange(virt_count, dtype=jnp.int32)
    first_live = positions < irrep_counts[0]
    second_live = positions < irrep_counts[1]
    window = jnp.concatenate([first_live, second_live])
    partner_live = lax.dynamic_slice_in_dim(
        window, lax.axis_index("tile") * width_inner, width_inner
    )
    orbital_live = lax.dynamic_slice_in_dim(
        second_live, lax.axis_index("sect") * width_outer, width_outer
    )
    nothing = jnp.zeros((), jnp.bfloat16)
    left_mat = jnp.where(partner_live[None, :, None] & first_live[None, None, :], left_all, nothing)
    left_mat = left_mat.reshape(aux_count, width_inner * virt_count)
    right_live = jnp.where(orbital_live[None, :, None] & window[None, None, :], chol_right, nothing)
    full_window = right_live.shape[2]

    def ladder_block(orbital):
        column = lax.dynamic_index_in_dim(right_live, orbital, 1, keepdims=False)
        coulomb = lax.dot_general(
            left_mat, column, (((0,), (0,)), ((), ())), preferred_element_type=jnp.float32
        )
        coulomb = coulomb.astype(jnp.bfloat16).reshape(width_inner, virt_count, full_window)
        return lax.dot_general(
            lam_all, coulomb, (((1, 2), (0, 2)), ((), ())), preferred_element_type=jnp.float32
        )

    orbitals = jnp.arange(width_outer, dtype=jnp.int32)
    stacked = lax.map(ladder_block, orbitals)
    summed = lax.psum_scatter(stacked, "tile", scatter_dimension=1, tiled=True)
    return jnp.transpose(summed, (1, 2, 0)).astype(jnp.bfloat16)


def solution(mesh):
    return jax.shard_map(
        per_device,
        mesh=mesh,
        in_specs=(P(), P("sect", "tile", None), P(None, "sect", None), P("sect", "tile", None)),
        out_specs=P("tile", None, "sect"),
        check_vma=False,
    )
```

profile of v0, /device:TPU:2, one launch (start us, length us, event | category | flops | bytes accessed | tf_op | source)
XLA Modules:
  0.0 434.3 jit_solution(6390705714932123795)
XLA Ops:
  11.1 10.7 %copy_select_fusion = bf16[896,16,256]{2,0,1:T(8,128)(2,1)} fusion(bf16[896,16,256]{2,1,0:T(8,128)(2,1)} %param.8, pred[16,256]{1,0:T(8,128)(4,1)S(1)} %broadcast_and_fusion), kind=kLoop, calls=%fused_computation.6 | loop fusion | flops 3670016 | bytes 14684160 | tf_op jit(solution)/shard_map/jit(_where)/select_n | solution.py:25
  21.8 33.9 %all-gather.3.cloned.1.call-done = bf16[896,8,128]{2,1,0:T(8,128)(2,1)} async-done(((bf16[112,8,128]{2,1,0:T(8,128)(2,1)}), bf16[896,8,128]{2,1,0:T(8,128)(2,1)}) %all-gather.3.cloned.1.call-update) | async-done | bytes 1835024 | tf_op jit(solution)/shard_map/all_gather | solution.py:8
  59.1 41.5 %all-gather.5.cloned.1.call-done = bf16[512,8,256]{2,1,0:T(8,128)(2,1)} async-done(((bf16[64,8,256]{2,1,0:T(8,128)(2,1)}), bf16[512,8,256]{2,1,0:T(8,128)(2,1)}) %all-gather.5.cloned.1.call-update) | async-done | bytes 2097168 | tf_op jit(solution)/shard_map/all_gather | solution.py:9
  100.6 3.8 copy.16
  104.5 223.7 %while.10 = (s32[]{:T(128)}, f32[16,512,128]{2,0,1:T(8,128)}, s32[16]{0:T(128)S(1)}, bf16[896,16,256]{2,0,1:T(8,128)(2,1)}, bf16[896,1024]{1,0:T(8,128)(2,1)}, /...) while((s32[]{:T(128)}, f32[16,512,128]{2,0,1:T(8,128)}, s32[16]{0:T(128)S(1)}, ...), condition=%wide.region_1.2_spmd, body=%wide.region_0.1_spmd.sunk | while | flops 738459648 | bytes 7798931 | solution.py:39
  110.4 8.1 %dynamic_update_slice.5 = f32[16,512,128]{2,0,1:T(8,128)} dynamic-update-slice(f32[16,512,128]{2,0,1:T(8,128)} %get-tuple-element.105, f32[1,512,128]{2,0,1:T(1,128)S(1)} %copy.28, s32[]{:T(128)} %get-tuple-element.104, s32[]{:T(128)} %constant.18.clone.1..sunk, s32[]{:T(128)} %constant.18.clone.1..sunk) | dynamic-update-slice | bytes 524292 | tf_op jit(solution)/shard_map/while/body/jit(dynamic_update_index_in_dim)/dynamic_update_slice | solution.py:39
  121.2 2.4 fusion.17
  124.3 8.1 %dynamic_update_slice.5 = f32[16,512,128]{2,0,1:T(8,128)} dynamic-update-slice(f32[16,512,128]{2,0,1:T(8,128)} %get-tuple-element.105, f32[1,512,128]{2,0,1:T(1,128)S(1)} %copy.28, s32[]{:T(128)} %get-tuple-element.104, s32[]{:T(128)} %constant.18.clone.1..sunk, s32[]{:T(128)} %constant.18.clone.1..sunk) | dynamic-update-slice | bytes 524292 | tf_op jit(solution)/shard_map/while/body/jit(dynamic_update_index_in_dim)/dynamic_update_slice | solution.py:39
  138.3 8.1 %dynamic_update_slice.5 = f32[16,512,128]{2,0,1:T(8,128)} dynamic-update-slice(f32[16,512,128]{2,0,1:T(8,128)} %get-tuple-element.105, f32[1,512,128]{2,0,1:T(1,128)S(1)} %copy.28, s32[]{:T(128)} %get-tuple-element.104, s32[]{:T(128)} %constant.18.clone.1..sunk, s32[]{:T(128)} %constant.18.clone.1..sunk) | dynamic-update-slice | bytes 524292 | tf_op jit(solution)/shard_map/while/body/jit(dynamic_update_index_in_dim)/dynamic_update_slice | solution.py:39
  152.3 8.1 %dynamic_update_slice.5 = f32[16,512,128]{2,0,1:T(8,128)} dynamic-update-slice(f32[16,512,128]{2,0,1:T(8,128)} %get-tuple-element.105, f32[1,512,128]{2,0,1:T(1,128)S(1)} %copy.28, s32[]{:T(128)} %get-tuple-element.104, s32[]{:T(128)} %constant.18.clone.1..sunk, s32[]{:T(128)} %constant.18.clone.1..sunk) | dynamic-update-slice | bytes 524292 | tf_op jit(solution)/shard_map/while/body/jit(dynamic_update_index_in_dim)/dynamic_update_slice | solution.py:39
  166.3 8.1 %dynamic_update_slice.5 = f32[16,512,128]{2,0,1:T(8,128)} dynamic-update-slice(f32[16,512,128]{2,0,1:T(8,128)} %get-tuple-element.105, f32[1,512,128]{2,0,1:T(1,128)S(1)} %copy.28, s32[]{:T(128)} %get-tuple-element.104, s32[]{:T(128)} %constant.18.clone.1..sunk, s32[]{:T(128)} %constant.18.clone.1..sunk) | dynamic-update-slice | bytes 524292 | tf_op jit(solution)/shard_map/while/body/jit(dynamic_update_index_in_dim)/dynamic_update_slice | solution.py:39
  177.1 2.4 fusion.17
  180.2 8.1 %dynamic_update_slice.5 = f32[16,512,128]{2,0,1:T(8,128)} dynamic-update-slice(f32[16,512,128]{2,0,1:T(8,128)} %get-tuple-element.105, f32[1,512,128]{2,0,1:T(1,128)S(1)} %copy.28, s32[]{:T(128)} %get-tuple-element.104, s32[]{:T(128)} %constant.18.clone.1..sunk, s32[]{:T(128)} %constant.18.clone.1..sunk) | dynamic-update-slice | bytes 524292 | tf_op jit(solution)/shard_map/while/body/jit(dynamic_update_index_in_dim)/dynamic_update_slice | solution.py:39
  194.2 8.1 %dynamic_update_slice.5 = f32[16,512,128]{2,0,1:T(8,128)} dynamic-update-slice(f32[16,512,128]{2,0,1:T(8,128)} %get-tuple-element.105, f32[1,512,128]{2,0,1:T(1,128)S(1)} %copy.28, s32[]{:T(128)} %get-tuple-element.104, s32[]{:T(128)} %constant.18.clone.1..sunk, s32[]{:T(128)} %constant.18.clone.1..sunk) | dynamic-update-slice | bytes 524292 | tf_op jit(solution)/shard_map/while/body/jit(dynamic_update_index_in_dim)/dynamic_update_slice | solution.py:39
  208.2 8.1 %dynamic_update_slice.5 = f32[16,512,128]{2,0,1:T(8,128)} dynamic-update-slice(f32[16,512,128]{2,0,1:T(8,128)} %get-tuple-element.105, f32[1,512,128]{2,0,1:T(1,128)S(1)} %copy.28, s32[]{:T(128)} %get-tuple-element.104, s32[]{:T(128)} %constant.18.clone.1..sunk, s32[]{:T(128)} %constant.18.clone.1..sunk) | dynamic-update-slice | bytes 524292 | tf_op jit(solution)/shard_map/while/body/jit(dynamic_update_index_in_dim)/dynamic_update_slice | solution.py:39
  222.1 8.1 %dynamic_update_slice.5 = f32[16,512,128]{2,0,1:T(8,128)} dynamic-update-slice(f32[16,512,128]{2,0,1:T(8,128)} %get-tuple-element.105, f32[1,512,128]{2,0,1:T(1,128)S(1)} %copy.28, s32[]{:T(128)} %get-tuple-element.104, s32[]{:T(128)} %constant.18.clone.1..sunk, s32[]{:T(128)} %constant.18.clone.1..sunk) | dynamic-update-slice | bytes 524292 | tf_op jit(solution)/shard_map/while/body/jit(dynamic_update_index_in_dim)/dynamic_update_slice | solution.py:39
  236.1 8.1 %dynamic_update_slice.5 = f32[16,512,128]{2,0,1:T(8,128)} dynamic-update-slice(f32[16,512,128]{2,0,1:T(8,128)} %get-tuple-element.105, f32[1,512,128]{2,0,1:T(1,128)S(1)} %copy.28, s32[]{:T(128)} %get-tuple-element.104, s32[]{:T(128)} %constant.18.clone.1..sunk, s32[]{:T(128)} %constant.18.clone.1..sunk) | dynamic-update-slice | bytes 524292 | tf_op jit(solution)/shard_map/while/body/jit(dynamic_update_index_in_dim)/dynamic_update_slice | solution.py:39
  250.1 8.1 %dynamic_update_slice.5 = f32[16,512,128]{2,0,1:T(8,128)} dynamic-update-slice(f32[16,512,128]{2,0,1:T(8,128)} %get-tuple-element.105, f32[1,512,128]{2,0,1:T(1,128)S(1)} %copy.28, s32[]{:T(128)} %get-tuple-element.104, s32[]{:T(128)} %constant.18.clone.1..sunk, s32[]{:T(128)} %constant.18.clone.1..sunk) | dynamic-update-slice | bytes 524292 | tf_op jit(solution)/shard_map/while/body/jit(dynamic_update_index_in_dim)/dynamic_update_slice | solution.py:39
  264.1 8.1 %dynamic_update_slice.5 = f32[16,512,128]{2,0,1:T(8,128)} dynamic-update-slice(f32[16,512,128]{2,0,1:T(8,128)} %get-tuple-element.105, f32[1,512,128]{2,0,1:T(1,128)S(1)} %copy.28, s32[]{:T(128)} %get-tuple-element.104, s32[]{:T(128)} %constant.18.clone.1..sunk, s32[]{:T(128)} %constant.18.clone.1..sunk) | dynamic-update-slice | bytes 524292 | tf_op jit(solution)/shard_map/while/body/jit(dynamic_update_index_in_dim)/dynamic_update_slice | solution.py:39
  278.1 8.1 %dynamic_update_slice.5 = f32[16,512,128]{2,0,1:T(8,128)} dynamic-update-slice(f32[16,512,128]{2,0,1:T(8,128)} %get-tuple-element.105, f32[1,512,128]{2,0,1:T(1,128)S(1)} %copy.28, s32[]{:T(128)} %get-tuple-element.104, s32[]{:T(128)} %constant.18.clone.1..sunk, s32[]{:T(128)} %constant.18.clone.1..sunk) | dynamic-update-slice | bytes 524292 | tf_op jit(solution)/shard_map/while/body/jit(dynamic_update_index_in_dim)/dynamic_update_slice | solution.py:39
  292.1 8.1 %dynamic_update_slice.5 = f32[16,512,128]{2,0,1:T(8,128)} dynamic-update-slice(f32[16,512,128]{2,0,1:T(8,128)} %get-tuple-element.105, f32[1,512,128]{2,0,1:T(1,128)S(1)} %copy.28, s32[]{:T(128)} %get-tuple-element.104, s32[]{:T(128)} %constant.18.clone.1..sunk, s32[]{:T(128)} %constant.18.clone.1..sunk) | dynamic-update-slice | bytes 524292 | tf_op jit(solution)/shard_map/while/body/jit(dynamic_update_index_in_dim)/dynamic_update_slice | solution.py:39
  306.1 8.1 %dynamic_update_slice.5 = f32[16,512,128]{2,0,1:T(8,128)} dynamic-update-slice(f32[16,512,128]{2,0,1:T(8,128)} %get-tuple-element.105, f32[1,512,128]{2,0,1:T(1,128)S(1)} %copy.28, s32[]{:T(128)} %get-tuple-element.104, s32[]{:T(128)} %constant.18.clone.1..sunk, s32[]{:T(128)} %constant.18.clone.1..sunk) | dynamic-update-slice | bytes 524292 | tf_op jit(solution)/shard_map/while/body/jit(dynamic_update_index_in_dim)/dynamic_update_slice | solution.py:39
  320.1 8.1 %dynamic_update_slice.5 = f32[16,512,128]{2,0,1:T(8,128)} dynamic-update-slice(f32[16,512,128]{2,0,1:T(8,128)} %get-tuple-element.105, f32[1,512,128]{2,0,1:T(1,128)S(1)} %copy.28, s32[]{:T(128)} %get-tuple-element.104, s32[]{:T(128)} %constant.18.clone.1..sunk, s32[]{:T(128)} %constant.18.clone.1..sunk) | dynamic-update-slice | bytes 524292 | tf_op jit(solution)/shard_map/while/body/jit(dynamic_update_index_in_dim)/dynamic_update_slice | solution.py:39
  328.2 98.0 %reduce-scatter.2.cloned.1.call-done = f32[16,16,128]{2,0,1:T(8,128)} async-done(((f32[16,512,128]{2,0,1:T(8,128)}), f32[16,16,128]{2,0,1:T(8,128)}) %reduce-scatter.2.cloned.1.call-update) | async-done | bytes 131088 | tf_op jit(solution)/shard_map/reduce_scatter | solution.py:40
  (97 shorter events, 65.3 us)
Async XLA Ops:
  6.5 49.2 %all-gather.3.cloned.1.call-start = ((), (), s32[]{:S(2)}) async-start(), calls=%async_computation.1 | async-start | bytes 2064384 | tf_op jit(solution)/shard_map/all_gather | solution.py:8
  7.3 93.3 %all-gather.5.cloned.1.call-start = ((), (), s32[]{:S(2)}) async-start(), calls=%async_computation.2 | async-start | bytes 2359296 | tf_op jit(solution)/shard_map/all_gather | solution.py:9
  8.0 418.2 %reduce-scatter.2.cloned.1.call-start = ((), (), s32[]{:S(2)}) async-start(), calls=%async_computation.3 | async-start | bytes 4325376 | tf_op jit(solution)/shard_map/reduce_scatter | solution.py:40
Sparse Core Ops, SparseCore 0:
  9.1 46.5 all-gather.2
  57.5 43.0 all-gather.4
  328.3 97.8 reduce-scatter.1
where the time goes:
time: 439 us; the launch traced here: 434 us
  waiting for transfers between devices  175 us (40%)
  local copies, waits for them, and re-layouts  151 us (34%)
  matrix products  46.6 us (11%)
  loops' own time  33.7 us (8%)
  other arithmetic  15.4 us (4%)
  between operations  13.2 us (3%)
    dynamic_update_slice x32, local copies, waits for them, and re-layouts, per_device(): stacked = lax.map(ladder_block, orbitals)  131 us
    reduce_scatter x1, waiting for transfers between devices, per_device(): summed = lax.psum_scatter(stacked, 'tile', scatter_dimension=1, tiled=True)  98 us
    all_gather x1, waiting for transfers between devices, per_device(): lam_all = lax.all_gather(lam, 'sect', axis=0, tiled=True)  41.5 us
    dot_general x16, matrix products, ladder_block(): lax.dot_general(left_mat, column, (((0,), (0,)), ((), ())), preferred_ele...  38.4 us
    all_gather x1, waiting for transfers between devices, per_device(): left_all = lax.all_gather(chol_left, 'sect', axis=0, tiled=True)  33.9 us
    another operation x1, loops' own time, per_device(): stacked = lax.map(ladder_block, orbitals)  33.7 us
    select_n x1, other arithmetic, per_device(): jnp.where(orbital_live[None, :, None] & window[None, None, :], chol_right...  10.7 us
    dynamic_slice x16, local copies, waits for them, and re-layouts, per_device(): stacked = lax.map(ladder_block, orbitals)  10.6 us
  transfers between devices with their start and end apart: 3, of which 3 were waited for; matrix products, arithmetic and copies ran while one was open for 4% of the time, Pallas kernels for 0%

commit v1 on v0

v1 whole, which is shorter than its diff:
```python
import functools

import jax
import jax.numpy as jnp
from jax import lax
from jax.experimental import pallas as pl
from jax.experimental.pallas import tpu as pltpu
from jax.sharding import PartitionSpec as P

MESH = pl.DeviceIdType.MESH
BF, F32 = jnp.bfloat16, jnp.float32
YN, XN, ZN = 4, 4, 4
SECTS = 2 * YN
QB, CB, AN, DN = 112, 8, 128, 256
QN = QB * SECTS
BN = 16
GROUPS, ROWS = 2, 32
RC, NB = 2, 4
STAGES = 14
STEP = QN // STAGES
Z_FIRST = (1, 1, 0, 1, 1, 0, 1, 0, 1, 1, 0, 1, 1, 0, 1, 0)
FAR_PLUS = (1, 0, 1, 0, 0, 1, 0, 1, 1, 0, 1, 0, 0, 1, 0, 1)


def kernel(counts, left, lam, right, out,
           lbuf, ltr, mbuf, rstage, rmat, coul, p32, pbf, rpair,
           s32, sbf, xfar, xfwd, xdir, u32, ubf, zfar, zfwd, zdir,
           rsem, ag_send, ag_recv, pr_send, pr_recv, x_send, x_recv, z_send, z_recv):
    sect, tile = lax.axis_index("sect"), lax.axis_index("tile")
    zl, y = sect // YN, sect % YN
    zh, x, core = tile // (2 * XN), (tile // 2) % XN, tile % 2
    base, obase = zl * YN, (1 - zl) * YN
    yp, ym, yf = (y + 1) % YN, (y + YN - 1) % YN, (y + 2) % YN
    at_yp, at_ym, at_z = {"sect": base + yp}, {"sect": base + ym}, {"sect": obase + y}

    def tile_at(zz, xx, cc):
        return {"tile": (zz * XN + xx) * 2 + cc}

    xp, xm, xf = (x + 1) % XN, (x + XN - 1) % XN, (x + 2) % XN
    zp, zm, zf = (zh + 1) % ZN, (zh + ZN - 1) % ZN, (zh + 2) % ZN
    at_xp, at_xm = tile_at(zh, xp, core), tile_at(zh, xm, core)
    at_zp, at_zm = tile_at(zp, x, core), tile_at(zm, x, core)
    at_pair = tile_at(zh, x, 1 - core)

    barrier = pltpu.get_barrier_semaphore()
    friends = (at_yp, at_ym, at_z, at_xp, at_xm, at_zp, at_zm, at_pair)
    for friend in friends:
        pl.semaphore_signal(barrier, inc=1, device_id=friend, device_id_type=MESH)

    def stage_copy(k):
        rows = pl.ds(k * STEP, STEP)
        return pltpu.make_async_copy(right.at[rows], rstage.at[rows], rsem.at[k])

    for k in range(STAGES):
        stage_copy(k).start()

    n1, n2 = counts[0], counts[1]
    own = pltpu.einshape("qca->cqa", left[...])
    lane = lax.broadcasted_iota(jnp.int32, (QB, AN), 1)
    for c in range(CB):
        orbital = tile * CB + c
        room = jnp.where(orbital < AN, n1 - orbital, n2 + AN - orbital)
        limit = jnp.where(room > 0, n1, 0)
        kept = jnp.where(lane < limit, own[c].astype(F32), 0.0).astype(BF)
        lbuf[c, pl.ds(pl.multiple_of(sect * QB, 16), QB), :] = kept
    lane = lax.broadcasted_iota(jnp.int32, (ROWS, DN), 1)
    d_live = lane < jnp.where(lane < AN, n1, n2 + AN)
    for g in range(GROUPS):
        mine = jnp.concatenate([lam[16 * u + 8 * g : 16 * u + 8 * g + 8] for u in range(4)], axis=0)
        mine = pltpu.einshape("icd->cid", mine)
        for c in range(CB):
            kept = jnp.where(d_live, mine[c].astype(F32), 0.0).astype(BF)
            mbuf[g, pl.ds(pl.multiple_of(sect * ROWS, 16), ROWS), c * DN : (c + 1) * DN] = kept

    sent = []

    def go(copy):
        copy.start()
        sent.append(copy)

    def piece(p, src):
        if p < 8:
            return lbuf.at[p, pl.ds(pl.multiple_of(src * QB, 16), QB), :]
        g, part = divmod(p - 8, 4)
        return mbuf.at[g, pl.ds(pl.multiple_of(src * ROWS, 16), ROWS), pl.ds(part * 2 * DN, 2 * DN)]

    def pass_on(p, src, k, where):
        ref = piece(p, src)
        go(pltpu.make_async_remote_copy(ref, ref, ag_send.at[p, k], ag_recv.at[p, src], where, MESH))

    def arrived(p, src):
        ref = piece(p, src)
        pltpu.make_async_remote_copy(ref, ref, ag_send.at[p, 0], ag_recv.at[p, src], at_z, MESH).wait_recv()

    def ag_own(p):
        if Z_FIRST[p]:
            pass_on(p, sect, 0, at_z)
        pass_on(p, sect, 1, at_yp)
        pass_on(p, sect, 2, at_ym)
        if not Z_FIRST[p]:
            pass_on(p, sect, 0, at_z)

    def ag_near(p):
        if Z_FIRST[p]:
            arrived(p, obase + y)
            pass_on(p, obase + y, 4, at_yp)
            pass_on(p, obase + y, 5, at_ym)
        arrived(p, base + ym)
        if FAR_PLUS[p]:
            pass_on(p, base + ym, 3, at_yp)
        if not Z_FIRST[p]:
            pass_on(p, base + ym, 4, at_z)
        arrived(p, base + yp)
        if not FAR_PLUS[p]:
            pass_on(p, base + yp, 3, at_ym)
        if not Z_FIRST[p]:
            pass_on(p, base + yp, 5, at_z)

    def ag_far(p):
        if Z_FIRST[p]:
            arrived(p, obase + ym)
            if FAR_PLUS[p]:
                pass_on(p, obase + ym, 6, at_yp)
            arrived(p, obase + yp)
            if not FAR_PLUS[p]:
                pass_on(p, obase + yp, 6, at_ym)
        else:
            arrived(p, base + yf)
            pass_on(p, base + yf, 6, at_z)

    def ag_end(p):
        if Z_FIRST[p]:
            arrived(p, base + yf)
            arrived(p, obase + yf)
        else:
            for other in (y, ym, yp, yf):
                arrived(p, obase + other)

    def relay(first, last):
        def body(k, carry):
            stage_copy(k).wait()
            rows = pl.ds(pl.multiple_of(k * STEP, 16), STEP)
            rmat[:, rows, :] = pltpu.einshape("qbd->bqd", rstage[rows])
            return carry

        lax.fori_loop(first, last, body, 0)

    def turn(h):
        for c in range(4 * h, 4 * h + 4):
            ltr[c * AN : (c + 1) * AN, :] = lbuf[c].T

    def coulomb(h, first, last):
        def body(b, carry):
            block = jnp.dot(ltr[h * 4 * AN : (h + 1) * 4 * AN, :], rmat[b], preferred_element_type=F32).astype(BF)
            for k in range(4):
                c = 4 * h + k
                coul[b, :, c * DN : (c + 1) * DN] = block[k * AN : (k + 1) * AN]
            return carry

        lax.fori_loop(first, last, body, 0)

    def ladder(g, r):
        def body(j, carry):
            pair = coul[pl.ds(2 * (r * NB + j), 2)].reshape(2 * AN, CB * DN)
            block = lax.dot_general(mbuf[g], pair, (((1,), (1,)), ((), ())), preferred_element_type=F32)
            block = block.reshape(ZN, XN, 2, 8, 2 * AN)
            block = jnp.concatenate([block[..., :AN], block[..., AN:]], axis=3)
            for cc in range(2):
                for xx in range(XN):
                    p32[g, r, cc, xx, :, j] = block[:, xx, cc]
                    pbf[g, r, cc, xx, :, j] = block[:, xx, cc].astype(BF)
            return carry

        lax.fori_loop(0, NB, body, 0)

    def pair_copy(g, r):
        return pltpu.make_async_remote_copy(
            pbf.at[g, r, 1 - core], rpair.at[g, r], pr_send.at[g, r], pr_recv.at[g, r], at_pair, MESH)

    def ring_copies(g, r, bf, far, fwd, direct, sends, recvs, cp, cm, cf, to_p, to_m):
        half = bf.shape[3] // 2
        lo, hi = pl.ds(0, half), pl.ds(half, half)
        ends = (
            (bf.at[g, r, cf, lo], far.at[g, r, 0], to_p),
            (bf.at[g, r, cf, hi], far.at[g, r, 1], to_m),
            (bf.at[g, r, cp, hi], direct.at[g, r, 0, hi], to_p),
            (bf.at[g, r, cm, lo], direct.at[g, r, 1, lo], to_m),
            (fwd.at[g, r, 0], direct.at[g, r, 0, lo], to_p),
            (fwd.at[g, r, 1], direct.at[g, r, 1, hi], to_m),
        )

        def copy(k):
            src, dst, where = ends[k]
            return pltpu.make_async_remote_copy(src, dst, sends.at[g, r, k], recvs.at[g, r, k], where, MESH)

        return copy

    def x_copies(g, r):
        return ring_copies(g, r, sbf, xfar, xfwd, xdir, x_send, x_recv, xp, xm, xf, at_xp, at_xm)

    def z_copies(g, r):
        return ring_copies(g, r, ubf, zfar, zfwd, zdir, z_send, z_recv, zp, zm, zf, at_zp, at_zm)

    def ring_mid(g, r, copies, total, far, fwd, cp, cm):
        half = total.shape[3] // 2
        copies(0).wait_recv()
        fwd[g, r, 0] = (total[g, r, cp, :half] + far[g, r, 0].astype(F32)).astype(BF)
        go(copies(4))
        copies(1).wait_recv()
        fwd[g, r, 1] = (total[g, r, cm, half:] + far[g, r, 1].astype(F32)).astype(BF)
        go(copies(5))

    def ring_end(g, r, copies, total, direct, me):
        for k in range(2, 6):
            copies(k).wait_recv()
        return total[g, r, me] + direct[g, r, 0].astype(F32) + direct[g, r, 1].astype(F32)

    def red1(g, r):
        ladder(g, r)
        go(pair_copy(g, r))

    def red2(g, r):
        pair_copy(g, r).wait_recv()
        for xx in range(XN):
            total = p32[g, r, core, xx] + rpair[g, r, xx].astype(F32)
            s32[g, r, xx] = total
            sbf[g, r, xx] = total.astype(BF)
        copies = x_copies(g, r)
        for k in range(4):
            go(copies(k))

    def red3(g, r):
        ring_mid(g, r, x_copies(g, r), s32, xfar, xfwd, xp, xm)

    def red4(g, r):
        total = ring_end(g, r, x_copies(g, r), s32, xdir, x)
        u32[g, r] = total
        ubf[g, r] = total.astype(BF)
        copies = z_copies(g, r)
        for k in range(4):
            go(copies(k))

    def red5(g, r):
        ring_mid(g, r, z_copies(g, r), u32, zfar, zfwd, zp, zm)

    def red6(g, r):
        out[g, r] = ring_end(g, r, z_copies(g, r), u32, zdir, zh)

    pl.semaphore_wait(barrier, len(friends))

    for p in range(8):
        ag_own(p)
    relay(0, 2)
    ag_near(0), ag_near(1)
    relay(2, 4)
    ag_near(2), ag_near(3)
    relay(4, 6)
    ag_near(4), ag_near(5), ag_far(0), ag_far(1)
    relay(6, 8)
    ag_near(6), ag_near(7), ag_far(2), ag_far(3)
    for p in range(8, 12):
        ag_own(p)
    relay(8, 10)
    ag_far(4), ag_far(5)
    relay(10, 12)
    ag_far(6), ag_far(7)
    relay(12, 14)
    for p in range(0, 4):
        ag_end(p)
    turn(0)
    coulomb(0, 0, 8)
    ag_near(8), ag_near(9)
    coulomb(0, 8, 16)
    ag_near(10), ag_near(11)
    for p in range(12, 16):
        ag_own(p)
    for p in range(4, 8):
        ag_end(p)
    turn(1)
    ag_far(8), ag_far(9)
    coulomb(1, 0, 8)
    ag_far(10), ag_far(11), ag_near(12), ag_near(13)
    coulomb(1, 8, 16)
    ag_near(14), ag_near(15)
    for p in range(8, 12):
        ag_end(p)
    red1(0, 0)
    ag_far(12), ag_far(13)
    red1(0, 1)
    ag_far(14), ag_far(15)
    red2(0, 0), red2(0, 1), red3(0, 0), red3(0, 1), red4(0, 0)
    for p in range(12, 16):
        ag_end(p)
    red1(1, 0)
    red4(0, 1)
    red1(1, 1)
    red5(0, 0), red5(0, 1)
    red2(1, 0), red2(1, 1)
    red6(0, 0), red6(0, 1)
    red3(1, 0), red3(1, 1), red4(1, 0), red4(1, 1), red5(1, 0), red5(1, 1), red6(1, 0), red6(1, 1)
    for copy in sent:
        copy.wait_send()


def per_device(irrep_counts, chol_left, chol_right, lam):
    whole = (GROUPS, RC)
    spot = (16, AN)
    vmem = pltpu.VMEM
    dma = pltpu.SemaphoreType.DMA
    summed = pl.pallas_call(
        kernel,
        out_shape=jax.ShapeDtypeStruct(whole + (NB,) + spot, F32),
        in_specs=[
            pl.BlockSpec(memory_space=pltpu.SMEM),
            pl.BlockSpec(memory_space=vmem),
            pl.BlockSpec(memory_space=vmem),
            pl.BlockSpec(memory_space=pl.ANY),
        ],
        out_specs=pl.BlockSpec(memory_space=vmem),
        scratch_shapes=[
            vmem((CB, QN, AN), BF),
            vmem((CB * AN, QN), BF),
            vmem((GROUPS, ROWS * SECTS, CB * DN), BF),
            vmem((QN, BN, DN), BF),
            vmem((BN, QN, DN), BF),
            vmem((BN, AN, CB * DN), BF),
            vmem(whole + (2, XN, ZN, NB) + spot, F32),
            vmem(whole + (2, XN, ZN, NB) + spot, BF),
            vmem(whole + (XN, ZN, NB) + spot, BF),
            vmem(whole + (XN, ZN, NB) + spot, F32),
            vmem(whole + (XN, ZN, NB) + spot, BF),
            vmem(whole + (2, ZN // 2, NB) + spot, BF),
            vmem(whole + (2, ZN // 2, NB) + spot, BF),
            vmem(whole + (2, ZN, NB) + spot, BF),
            vmem(whole + (ZN, NB) + spot, F32),
            vmem(whole + (ZN, NB) + spot, BF),
            vmem(whole + (2, NB // 2) + spot, BF),
            vmem(whole + (2, NB // 2) + spot, BF),
            vmem(whole + (2, NB) + spot, BF),
            dma((STAGES,)),
            dma((16, 7)),
            dma((16, SECTS)),
            dma(whole),
            dma(whole),
            dma(whole + (6,)),
            dma(whole + (6,)),
            dma(whole + (6,)),
            dma(whole + (6,)),
        ],
        compiler_params=pltpu.CompilerParams(
            collective_id=0, has_side_effects=True, vmem_limit_bytes=56 << 20
        ),
        cost_estimate=pl.CostEstimate(flops=12_000_000_000, bytes_accessed=8_000_000, transcendentals=0),
    )(irrep_counts, chol_left, lam, chol_right)
    summed = summed.reshape(GROUPS, RC, NB, 2, 8, AN)
    summed = jnp.transpose(summed, (0, 4, 5, 1, 2, 3)).reshape(GROUPS * 8, AN, BN)
    orbital = lax.axis_index("sect") * BN + lax.broadcasted_iota(jnp.int32, summed.shape, 2)
    return jnp.where(orbital < irrep_counts[1], summed, 0.0).astype(BF)


def solution(mesh):
    return jax.shard_map(
        per_device,
        mesh=mesh,
        in_specs=(P(), P("sect", "tile", None), P(None, "sect", None), P("sect", "tile", None)),
        out_specs=P("tile", None, "sect"),
        check_vma=False,
    )
```

time: 439 us -> 79.1 us (0.18); the launches traced: 434 us -> 78.9 us
  waiting for transfers between devices: 175 us -> 0 us
  local copies, waits for them, and re-layouts: 151 us -> 1.56 us
  Pallas kernels: 0 us -> 76 us
  matrix products: 46.6 us -> 0 us
  loops' own time: 33.7 us -> 0 us
  other arithmetic: 15.4 us -> 1.36 us
  between operations: 13.2 us -> 0.03 us
    dynamic_update_slice x32 -> x0, local copies, waits for them, and re-layouts: 131 us -> none  [per_device(): stacked = lax.map(ladder_block, orbitals)]
    reduce_scatter x1 -> x0, waiting for transfers between devices: 98 us -> none  [per_device(): summed = lax.psum_scatter(stacked, 'tile', scatter_dimension=1, tiled=True)]
    pallas_call x0 -> x1, Pallas kernels: none -> 76 us  [per_device(): pl.pallas_call(kernel, out_shape=jax.ShapeDtypeStruct(whole + (NB,) + spo...]
    all_gather x2 -> x0, waiting for transfers between devices: 75.4 us -> none  [the longest x1 41.5 us: per_device(): lam_all = lax.all_gather(lam, 'sect', axis=0, tiled=True)]
    dot_general x32 -> x0, matrix products: 46.6 us -> none  [the longest x16 38.4 us: ladder_block(): lax.dot_general(left_mat, column, (((0,), (0,)), ((), ())), preferred_ele...]
    another operation x1 -> x0, loops' own time: 33.7 us -> none  [per_device(): stacked = lax.map(ladder_block, orbitals)]
    select_n x2 -> x0, other arithmetic: 12.4 us -> none  [the longest x1 10.7 us: per_device(): jnp.where(orbital_live[None, :, None] & window[None, None, :], chol_right...]
    dynamic_slice x18 -> x0, local copies, waits for them, and re-layouts: 10.8 us -> none  [the longest x16 10.6 us: per_device(): stacked = lax.map(ladder_block, orbitals)]
  transfers between devices with their start and end apart: 3 -> 0, of which waited for: 3 -> 0; matrix products, arithmetic and copies ran while one was open for 4% -> 0% of each run, Pallas kernels for 0% -> 0%
where the time goes in v1:
time: 79.1 us; the launch traced here: 78.9 us
  Pallas kernels  76 us (96%)
  local copies, waits for them, and re-layouts  1.56 us (2%)
  other arithmetic  1.36 us (2%)
    pallas_call x1, Pallas kernels, per_device(): pl.pallas_call(kernel, out_shape=jax.ShapeDtypeStruct(whole + (NB,) + spo...  76 us

profile of v1, /device:TPU:2, one launch (start us, length us, event | category | flops | bytes accessed | tf_op | source)
XLA Modules:
  0.0 78.9 jit_solution(8544771211962787568)
XLA Ops:
  0.0 0.0 copy-start
  0.0 76.0 %shard_map.46 = f32[2,2,4,16,128]{4,3,2,1,0:T(8,128)} custom-call(s32[2]{0:T(128)} %counts.1, bf16[112,8,128]{2,1,0:T(8,128)(2,1)} %left.1, bf16[64,8,256]{2,1,0:T(8,128)(2,1)} %lam.1, bf16[896,16,256]{2,1,0:T(8,128)(2,1)} %right.1), custom_call_target="tpu_custom_call" | custom-call | flops 12000000000 | bytes 8000000 | tf_op jit(solution)/shard_map/pallas_call | solution.py:310
  76.0 1.0 %copy.5 = bf16[2,8,128,2,4,2]{2,5,4,3,1,0:T(2,128)(2,1)S(1)} copy(f32[2,8,128,2,4,2]{2,1,5,4,3,0:T(8,128)} %bitcast.6) | data formatting | bytes 196608 | tf_op jit(solution)/shard_map/transpose | solution.py:356
  77.0 0.0 copy-done
  77.0 0.6 slice.3
  77.6 0.7 add_compare_fusion
  78.2 0.7 select_convert_fusion
Async XLA Ops:
  0.0 77.0 %copy-start = (s32[2]{0:T(128)S(1)}, s32[2]{0:T(128)}, u32[]{:S(2)}) copy-start(s32[2]{0:T(128)} %counts.1) | copy-start | bytes 28

commit v2 on v1

--- a/solution.py
+++ b/solution.py
@@ -18,20 +18,23 @@
 RC, NB = 2, 4
 STAGES = 14
 STEP = QN // STAGES
-Z_FIRST = (1, 1, 0, 1, 1, 0, 1, 0, 1, 1, 0, 1, 1, 0, 1, 0)
-FAR_PLUS = (1, 0, 1, 0, 0, 1, 0, 1, 1, 0, 1, 0, 0, 1, 0, 1)
+Z_FIRST = (1, 0, 1, 0, 1, 0, 0, 0, 1, 1, 1, 1, 0, 0, 1, 1)
+FAR_PLUS = (0, 1, 1, 0, 1, 0, 1, 1, 0, 0, 1, 1, 1, 0, 1, 0)
 
 
 def kernel(counts, left, lam, right, out,
            lbuf, ltr, mbuf, rstage, rmat, coul, p32, pbf, rpair,
            s32, sbf, xfar, xfwd, xdir, u32, ubf, zfar, zfwd, zdir,
-           rsem, ag_send, ag_recv, pr_send, pr_recv, x_send, x_recv, z_send, z_recv):
+           v32, acc, rsem, ag_send, ag_recv, pr_send, pr_recv, x_send, x_recv, z_send, z_recv):
     sect, tile = lax.axis_index("sect"), lax.axis_index("tile")
     zl, y = sect // YN, sect % YN
     zh, x, core = tile // (2 * XN), (tile // 2) % XN, tile % 2
     base, obase = zl * YN, (1 - zl) * YN
     yp, ym, yf = (y + 1) % YN, (y + YN - 1) % YN, (y + 2) % YN
     at_yp, at_ym, at_z = {"sect": base + yp}, {"sect": base + ym}, {"sect": obase + y}
+
+    bm, bp, bf = base + ym, base + yp, base + yf
+    oy, om, op, of = obase + y, obase + ym, obase + yp, obase + yf
 
     def tile_at(zz, xx, cc):
         return {"tile": (zz * XN + xx) * 2 + cc}
@@ -74,9 +77,9 @@
 
     sent = []
 
-    def go(copy):
-        copy.start()
-        sent.append(copy)
+    def go(make):
+        make().start()
+        sent.append(make)
 
     def piece(p, src):
         if p < 8:
@@ -85,8 +88,11 @@
         return mbuf.at[g, pl.ds(pl.multiple_of(src * ROWS, 16), ROWS), pl.ds(part * 2 * DN, 2 * DN)]
 
     def pass_on(p, src, k, where):
-        ref = piece(p, src)
-        go(pltpu.make_async_remote_copy(ref, ref, ag_send.at[p, k], ag_recv.at[p, src], where, MESH))
+        def make():
+            ref = piece(p, src)
+            return pltpu.make_async_remote_copy(ref, ref, ag_send.at[p, k], ag_recv.at[p, src], where, MESH)
+
+        go(make)
 
     def arrived(p, src):
         ref = piece(p, src)
@@ -102,76 +108,99 @@
 
     def ag_near(p):
         if Z_FIRST[p]:
-            arrived(p, obase + y)
-            pass_on(p, obase + y, 4, at_yp)
-            pass_on(p, obase + y, 5, at_ym)
-        arrived(p, base + ym)
+            arrived(p, oy)
+            pass_on(p, oy, 4, at_yp)
+            pass_on(p, oy, 5, at_ym)
+        arrived(p, bm)
         if FAR_PLUS[p]:
-            pass_on(p, base + ym, 3, at_yp)
+            pass_on(p, bm, 3, at_yp)
         if not Z_FIRST[p]:
-            pass_on(p, base + ym, 4, at_z)
-        arrived(p, base + yp)
+            pass_on(p, bm, 4, at_z)
+        arrived(p, bp)
         if not FAR_PLUS[p]:
-            pass_on(p, base + yp, 3, at_ym)
+            pass_on(p, bp, 3, at_ym)
         if not Z_FIRST[p]:
-            pass_on(p, base + yp, 5, at_z)
+            pass_on(p, bp, 5, at_z)
 
     def ag_far(p):
         if Z_FIRST[p]:
-            arrived(p, obase + ym)
+            arrived(p, om)
             if FAR_PLUS[p]:
-                pass_on(p, obase + ym, 6, at_yp)
-            arrived(p, obase + yp)
+                pass_on(p, om, 6, at_yp)
+            arrived(p, op)
             if not FAR_PLUS[p]:
-                pass_on(p, obase + yp, 6, at_ym)
+                pass_on(p, op, 6, at_ym)
         else:
-            arrived(p, base + yf)
-            pass_on(p, base + yf, 6, at_z)
+            arrived(p, bf)
+            pass_on(p, bf, 6, at_z)
 
     def ag_end(p):
         if Z_FIRST[p]:
-            arrived(p, base + yf)
-            arrived(p, obase + yf)
+            arrived(p, bf)
+            arrived(p, of)
         else:
-            for other in (y, ym, yp, yf):
-                arrived(p, obase + other)
-
-    def relay(first, last):
-        def body(k, carry):
+            for src in (oy, om, op, of):
+                arrived(p, src)
+
+    def loop(count, body, events):
+        def step(j, carry):
+            body(j)
+            for k, todo in events.items():
+                pl.when(j == k)(functools.partial(run, todo))
+            return carry
+
+        lax.fori_loop(0, count, step, 0)
+
+    def run(todo):
+        for name, *where in todo:
+            ACTIONS[name](*where)
+
+    def relay(events):
+        def body(k):
             stage_copy(k).wait()
             rows = pl.ds(pl.multiple_of(k * STEP, 16), STEP)
             rmat[:, rows, :] = pltpu.einshape("qbd->bqd", rstage[rows])
-            return carry
-
-        lax.fori_loop(first, last, body, 0)
+
+        loop(STAGES, body, events)
 
     def turn(h):
         for c in range(4 * h, 4 * h + 4):
             ltr[c * AN : (c + 1) * AN, :] = lbuf[c].T
 
-    def coulomb(h, first, last):
-        def body(b, carry):
-            block = jnp.dot(ltr[h * 4 * AN : (h + 1) * 4 * AN, :], rmat[b], preferred_element_type=F32).astype(BF)
-            for k in range(4):
-                c = 4 * h + k
-                coul[b, :, c * DN : (c + 1) * DN] = block[k * AN : (k + 1) * AN]
-            return carry
-
-        lax.fori_loop(first, last, body, 0)
-
-    def ladder(g, r):
-        def body(j, carry):
-            pair = coul[pl.ds(2 * (r * NB + j), 2)].reshape(2 * AN, CB * DN)
-            block = lax.dot_general(mbuf[g], pair, (((1,), (1,)), ((), ())), preferred_element_type=F32)
-            block = block.reshape(ZN, XN, 2, 8, 2 * AN)
-            block = jnp.concatenate([block[..., :AN], block[..., AN:]], axis=3)
-            for cc in range(2):
-                for xx in range(XN):
-                    p32[g, r, cc, xx, :, j] = block[:, xx, cc]
-                    pbf[g, r, cc, xx, :, j] = block[:, xx, cc].astype(BF)
-            return carry
-
-        lax.fori_loop(0, NB, body, 0)
+    def coulomb(h, events):
+        def body(j):
+            for b in (2 * j, 2 * j + 1):
+                block = jnp.dot(ltr[h * 4 * AN : (h + 1) * 4 * AN, :], rmat[b], preferred_element_type=F32).astype(BF)
+                for k in range(4):
+                    c = 4 * h + k
+                    coul[b, :, c * DN : (c + 1) * DN] = block[k * AN : (k + 1) * AN]
+
+        loop(BN // 2, body, events)
+
+    def product(g, quad, first, last):
+        cols = coul[pl.ds(4 * quad, 4), :, first * DN : last * DN].reshape(4 * AN, (last - first) * DN)
+        rows = mbuf[g, :, first * DN : last * DN]
+        return lax.dot_general(rows, cols, (((1,), (1,)), ((), ())), preferred_element_type=F32)
+
+    def early(g, events):
+        def body(quad):
+            acc[quad] = product(g, quad, 0, CB // 2)
+
+        loop(BN // 4, body, events)
+
+    def ladder(g, r, events):
+        def body(k):
+            quad = r * (NB // 2) + k
+            block = product(g, quad, 0, CB) if g == 0 else acc[quad] + product(g, quad, CB // 2, CB)
+            for m in range(2):
+                part = block[:, 2 * AN * m : 2 * AN * (m + 1)].reshape(ZN, XN, 2, 8, 2 * AN)
+                part = jnp.concatenate([part[..., :AN], part[..., AN:]], axis=3)
+                for cc in range(2):
+                    for xx in range(XN):
+                        p32[g, r, cc, xx, :, 2 * k + m] = part[:, xx, cc]
+                        pbf[g, r, cc, xx, :, 2 * k + m] = part[:, xx, cc].astype(BF)
+
+        loop(NB // 2, body, events)
 
     def pair_copy(g, r):
         return pltpu.make_async_remote_copy(
@@ -201,14 +230,15 @@
     def z_copies(g, r):
         return ring_copies(g, r, ubf, zfar, zfwd, zdir, z_send, z_recv, zp, zm, zf, at_zp, at_zm)
 
-    def ring_mid(g, r, copies, total, far, fwd, cp, cm):
+    def ring_mid(g, r, ring, total, far, fwd, cp, cm):
         half = total.shape[3] // 2
+        copies = ring(g, r)
         copies(0).wait_recv()
         fwd[g, r, 0] = (total[g, r, cp, :half] + far[g, r, 0].astype(F32)).astype(BF)
-        go(copies(4))
+        go(lambda: ring(g, r)(4))
         copies(1).wait_recv()
         fwd[g, r, 1] = (total[g, r, cm, half:] + far[g, r, 1].astype(F32)).astype(BF)
-        go(copies(5))
+        go(lambda: ring(g, r)(5))
 
     def ring_end(g, r, copies, total, direct, me):
         for k in range(2, 6):
@@ -216,8 +246,7 @@
         return total[g, r, me] + direct[g, r, 0].astype(F32) + direct[g, r, 1].astype(F32)
 
     def red1(g, r):
-        ladder(g, r)
-        go(pair_copy(g, r))
+        go(functools.partial(pair_copy, g, r))
 
     def red2(g, r):
         pair_copy(g, r).wait_recv()
@@ -225,81 +254,63 @@
             total = p32[g, r, core, xx] + rpair[g, r, xx].astype(F32)
             s32[g, r, xx] = total
             sbf[g, r, xx] = total.astype(BF)
-        copies = x_copies(g, r)
         for k in range(4):
-            go(copies(k))
+            go(functools.partial(lambda k: x_copies(g, r)(k), k))
 
     def red3(g, r):
-        ring_mid(g, r, x_copies(g, r), s32, xfar, xfwd, xp, xm)
+        ring_mid(g, r, x_copies, s32, xfar, xfwd, xp, xm)
 
     def red4(g, r):
         total = ring_end(g, r, x_copies(g, r), s32, xdir, x)
         u32[g, r] = total
         ubf[g, r] = total.astype(BF)
-        copies = z_copies(g, r)
         for k in range(4):
-            go(copies(k))
+            go(functools.partial(lambda k: z_copies(g, r)(k), k))
 
     def red5(g, r):
-        ring_mid(g, r, z_copies(g, r), u32, zfar, zfwd, zp, zm)
+        ring_mid(g, r, z_copies, u32, zfar, zfwd, zp, zm)
 
     def red6(g, r):
-        out[g, r] = ring_end(g, r, z_copies(g, r), u32, zdir, zh)
+        v32[g, r * NB : (r + 1) * NB] = ring_end(g, r, z_copies(g, r), u32, zdir, zh)
+
+    def finish(g):
+        summed = pltpu.einshape("bia->iba", v32[g].reshape(BN, 8, AN))
+        orbital = sect * BN + lax.broadcasted_iota(jnp.int32, summed.shape, 1)
+        out[8 * g : 8 * g + 8] = jnp.where(orbital < n2, summed, 0.0).astype(BF)
+
+    ACTIONS = dict(o=ag_own, n=ag_near, f=ag_far, e=ag_end, r1=red1, r2=red2, r3=red3, r4=red4, r5=red5, r6=red6, end=finish)
 
     pl.semaphore_wait(barrier, len(friends))
 
-    for p in range(8):
-        ag_own(p)
-    relay(0, 2)
-    ag_near(0), ag_near(1)
-    relay(2, 4)
-    ag_near(2), ag_near(3)
-    relay(4, 6)
-    ag_near(4), ag_near(5), ag_far(0), ag_far(1)
-    relay(6, 8)
-    ag_near(6), ag_near(7), ag_far(2), ag_far(3)
-    for p in range(8, 12):
-        ag_own(p)
-    relay(8, 10)
-    ag_far(4), ag_far(5)
-    relay(10, 12)
-    ag_far(6), ag_far(7)
-    relay(12, 14)
-    for p in range(0, 4):
-        ag_end(p)
+    def act(text):
+        words = text.split()
+        return [(w[:2], int(w[2]), int(w[3])) if w[0] == "r" else (w[0], int(w[1:])) for w in words]
+
+    run(act("o0 o1 o2 o3 o4"))
+    relay({7: act("o5 n0"), 9: act("n1"), 10: act("n2"), 12: act("n3")})
+    run(act("n4 n5 f0 o6 f1 o7 f2 f3 o8 f4 o9 f5 o10 o11 n6 n7 o12 e0 e1 e2 e3"))
     turn(0)
-    coulomb(0, 0, 8)
-    ag_near(8), ag_near(9)
-    coulomb(0, 8, 16)
-    ag_near(10), ag_near(11)
-    for p in range(12, 16):
-        ag_own(p)
-    for p in range(4, 8):
-        ag_end(p)
+    run(act("o13"))
+    coulomb(0, {0: act("o14 n8 n9"), 2: act("n10 f6 n11 f7"), 3: act("n12"), 4: act("n13"), 5: act("o15 f8"), 6: act("f9 n14 f10")})
+    run(act("e4 e5 e6 e7"))
     turn(1)
-    ag_far(8), ag_far(9)
-    coulomb(1, 0, 8)
-    ag_far(10), ag_far(11), ag_near(12), ag_near(13)
-    coulomb(1, 8, 16)
-    ag_near(14), ag_near(15)
-    for p in range(8, 12):
-        ag_end(p)
-    red1(0, 0)
-    ag_far(12), ag_far(13)
-    red1(0, 1)
-    ag_far(14), ag_far(15)
-    red2(0, 0), red2(0, 1), red3(0, 0), red3(0, 1), red4(0, 0)
-    for p in range(12, 16):
-        ag_end(p)
-    red1(1, 0)
-    red4(0, 1)
-    red1(1, 1)
-    red5(0, 0), red5(0, 1)
-    red2(1, 0), red2(1, 1)
-    red6(0, 0), red6(0, 1)
-    red3(1, 0), red3(1, 1), red4(1, 0), red4(1, 1), red5(1, 0), red5(1, 1), red6(1, 0), red6(1, 1)
-    for copy in sent:
-        copy.wait_send()
+    run(act("f11 f13"))
+    coulomb(1, {1: act("f12"), 2: act("f14"), 3: act("n15")})
+    run(act("e8 e9 e10 e11"))
+    ladder(0, 0, {0: act("f15")})
+    run(act("r100"))
+    ladder(0, 1, {})
+    run(act("r101 r200 e12 e13"))
+    early(1, {2: act("r201")})
+    run(act("e14 e15"))
+    ladder(1, 0, {})
+    run(act("r110 r300"))
+    ladder(1, 1, {})
+    run(act("r111 r301 r210 r211 r400 r401 r310 r311 r500 r501 r410 r411 r600 r601 r510 r511 r610 r611"))
+    finish(0)
+    finish(1)
+    for make in sent:
+        make().wait_send()
 
 
 def per_device(irrep_counts, chol_left, chol_right, lam):
@@ -309,7 +320,7 @@
     dma = pltpu.SemaphoreType.DMA
     summed = pl.pallas_call(
         kernel,
-        out_shape=jax.ShapeDtypeStruct(whole + (NB,) + spot, F32),
+        out_shape=jax.ShapeDtypeStruct((GROUPS * 8, BN, AN), BF),
         in_specs=[
             pl.BlockSpec(memory_space=pltpu.SMEM),
             pl.BlockSpec(memory_space=vmem),
@@ -337,6 +348,8 @@
             vmem(whole + (2, NB // 2) + spot, BF),
             vmem(whole + (2, NB // 2) + spot, BF),
             vmem(whole + (2, NB) + spot, BF),
+            vmem((GROUPS, RC * NB) + spot, F32),
+            vmem((BN // 4, ROWS * SECTS, 4 * AN), F32),
             dma((STAGES,)),
             dma((16, 7)),
             dma((16, SECTS)),
@@ -352,10 +365,7 @@
         ),
         cost_estimate=pl.CostEstimate(flops=12_000_000_000, bytes_accessed=8_000_000, transcendentals=0),
     )(irrep_counts, chol_left, lam, chol_right)
-    summed = summed.reshape(GROUPS, RC, NB, 2, 8, AN)
-    summed = jnp.transpose(summed, (0, 4, 5, 1, 2, 3)).reshape(GROUPS * 8, AN, BN)
-    orbital = lax.axis_index("sect") * BN + lax.broadcasted_iota(jnp.int32, summed.shape, 2)
-    return jnp.where(orbital < irrep_counts[1], summed, 0.0).astype(BF)
+    return jnp.transpose(summed, (0, 2, 1))
 
 
 def solution(mesh):

time: 79.1 us -> 67.3 us (0.85)
  Pallas kernels: 76 us -> 65.7 us
  other arithmetic: 1.36 us -> 0 us
    pallas_call x1, Pallas kernels: 76 us -> 65.7 us  [per_device(): pl.pallas_call(kernel, out_shape=jax.ShapeDtypeStruct((GROUPS * 8, BN, AN...]
    unnamed x2 -> x1, local copies, waits for them, and re-layouts: 0.01 us -> 1.47 us
    transpose x1 -> x0, local copies, waits for them, and re-layouts: 0.97 us -> none  [per_device(): jnp.transpose(summed, (0, 4, 5, 1, 2, 3)).reshape(GROUPS * 8, AN, BN)]
where the time goes in v2:
time: 67.3 us; the launch traced here: 67.2 us
  Pallas kernels  65.7 us (98%)
  local copies, waits for them, and re-layouts  1.47 us (2%)
    pallas_call x1, Pallas kernels, per_device(): pl.pallas_call(kernel, out_shape=jax.ShapeDtypeStruct((GROUPS * 8, BN, AN...  65.7 us
    unnamed x1, local copies, waits for them, and re-layouts  1.47 us

profile of v2, /device:TPU:2, one launch (start us, length us, event | category | flops | bytes accessed | tf_op | source)
XLA Modules:
  0.0 67.2 jit_solution(3985235192716024926)
XLA Ops:
  0.0 65.7 %shard_map.46 = bf16[16,16,128]{2,1,0:T(8,128)(2,1)} custom-call(s32[2]{0:T(128)} %counts.1, bf16[112,8,128]{2,1,0:T(8,128)(2,1)} %left.1, bf16[64,8,256]{2,1,0:T(8,128)(2,1)} %lam.1, bf16[896,16,256]{2,1,0:T(8,128)(2,1)} %right.1), custom_call_target="tpu_custom_call" | custom-call | flops 12000000000 | bytes 8000000 | tf_op jit(solution)/shard_map/pallas_call | solution.py:321
  65.7 1.5 %copy.6 = bf16[16,128,16]{1,2,0:T(8,128)(2,1)} copy(bf16[16,128,16]{1,2,0:T(8,128)(2,1)} %bitcast.1) | data formatting | bytes 131072

commit v3 on v2

--- a/solution.py
+++ b/solution.py
@@ -15,17 +15,18 @@
 QN = QB * SECTS
 BN = 16
 GROUPS, ROWS = 2, 32
+BLOCK = 4
 RC, NB = 2, 4
 STAGES = 14
 STEP = QN // STAGES
-Z_FIRST = (1, 0, 1, 0, 1, 0, 0, 0, 1, 1, 1, 1, 0, 0, 1, 1)
-FAR_PLUS = (0, 1, 1, 0, 1, 0, 1, 1, 0, 0, 1, 1, 1, 0, 1, 0)
+Z_FIRST = (0, 0, 0, 1, 1, 1, 1, 0, 1, 0, 0, 1, 0, 1, 1, 1)
+FAR_PLUS = (0, 1, 0, 1, 1, 1, 0, 0, 1, 1, 0, 1, 0, 1, 1, 0)
 
 
 def kernel(counts, left, lam, right, out,
-           lbuf, ltr, mbuf, rstage, rmat, coul, p32, pbf, rpair,
+           lbuf, ltra, ltrb, ltr, mbuf, rstage, rmat, coul, p32, pbf, rpair,
            s32, sbf, xfar, xfwd, xdir, u32, ubf, zfar, zfwd, zdir,
-           v32, acc, rsem, ag_send, ag_recv, pr_send, pr_recv, x_send, x_recv, z_send, z_recv):
+           v32, acc, acc0, rsem, ag_send, ag_recv, pr_send, pr_recv, x_send, x_recv, z_send, z_recv):
     sect, tile = lax.axis_index("sect"), lax.axis_index("tile")
     zl, y = sect // YN, sect % YN
     zh, x, core = tile // (2 * XN), (tile // 2) % XN, tile % 2
@@ -134,26 +135,31 @@
             arrived(p, bf)
             pass_on(p, bf, 6, at_z)
 
+    def ag_half(p):
+        if Z_FIRST[p]:
+            arrived(p, bf)
+
     def ag_end(p):
         if Z_FIRST[p]:
-            arrived(p, bf)
+            if p >= 4:
+                arrived(p, bf)
             arrived(p, of)
         else:
             for src in (oy, om, op, of):
                 arrived(p, src)
 
+    def run(*todo):
+        for event in todo:
+            event()
+
     def loop(count, body, events):
         def step(j, carry):
             body(j)
             for k, todo in events.items():
-                pl.when(j == k)(functools.partial(run, todo))
+                pl.when(j == k)(functools.partial(run, *todo))
             return carry
 
         lax.fori_loop(0, count, step, 0)
-
-    def run(todo):
-        for name, *where in todo:
-            ACTIONS[name](*where)
 
     def relay(events):
         def body(k):
@@ -163,33 +169,61 @@
 
         loop(STAGES, body, events)
 
-    def turn(h):
-        for c in range(4 * h, 4 * h + 4):
-            ltr[c * AN : (c + 1) * AN, :] = lbuf[c].T
-
-    def coulomb(h, events):
+    def layer(which):
+        return pl.ds(pl.multiple_of(which * (QN // 2), 16), QN // 2)
+
+    def turn_a():
+        for c in range(4):
+            ltra[c * AN : (c + 1) * AN, :] = lbuf[c, layer(zl), :].T
+
+    def turn_b():
+        for c in range(4):
+            ltrb[c * AN : (c + 1) * AN, :] = lbuf[c, layer(1 - zl), :].T
+
+    def turn_1():
+        for c in range(4):
+            ltr[c * AN : (c + 1) * AN, :] = lbuf[4 + c].T
+
+    def keep(b, first, block):
+        for k in range(4):
+            c = first + k
+            coul[b, :, c * DN : (c + 1) * DN] = block[k * AN : (k + 1) * AN].astype(BF)
+
+    def coulomb_a(events):
         def body(j):
-            for b in (2 * j, 2 * j + 1):
-                block = jnp.dot(ltr[h * 4 * AN : (h + 1) * 4 * AN, :], rmat[b], preferred_element_type=F32).astype(BF)
-                for k in range(4):
-                    c = 4 * h + k
-                    coul[b, :, c * DN : (c + 1) * DN] = block[k * AN : (k + 1) * AN]
-
-        loop(BN // 2, body, events)
+            for k in range(BLOCK):
+                b = BLOCK * j + k
+                acc0[b] = jnp.dot(ltra[...], rmat[b, layer(zl), :], preferred_element_type=F32)
+
+        loop(BN // BLOCK, body, events)
+
+    def coulomb_b(events):
+        def body(j):
+            for k in range(BLOCK):
+                b = BLOCK * j + k
+                keep(b, 0, acc0[b] + jnp.dot(ltrb[...], rmat[b, layer(1 - zl), :], preferred_element_type=F32))
+
+        loop(BN // BLOCK, body, events)
+
+    def coulomb_1(events):
+        def body(j):
+            for k in range(BLOCK):
+                b = BLOCK * j + k
+                keep(b, 4, jnp.dot(ltr[...], rmat[b], preferred_element_type=F32))
+
+        loop(BN // BLOCK, body, events)
 
     def product(g, quad, first, last):
-        cols = coul[pl.ds(4 * quad, 4), :, first * DN : last * DN].reshape(4 * AN, (last - first) * DN)
+        cols = coul[4 * quad : 4 * quad + 4, :, first * DN : last * DN].reshape(4 * AN, (last - first) * DN)
         rows = mbuf[g, :, first * DN : last * DN]
         return lax.dot_general(rows, cols, (((1,), (1,)), ((), ())), preferred_element_type=F32)
 
-    def early(g, events):
-        def body(quad):
-            acc[quad] = product(g, quad, 0, CB // 2)
-
-        loop(BN // 4, body, events)
-
-    def ladder(g, r, events):
-        def body(k):
+    def early():
+        for quad in range(BN // 4):
+            acc[quad] = product(1, quad, 0, CB // 2)
+
+    def ladder(g, r):
+        for k in range(NB // 2):
             quad = r * (NB // 2) + k
             block = product(g, quad, 0, CB) if g == 0 else acc[quad] + product(g, quad, CB // 2, CB)
             for m in range(2):
@@ -199,8 +233,6 @@
                     for xx in range(XN):
                         p32[g, r, cc, xx, :, 2 * k + m] = part[:, xx, cc]
                         pbf[g, r, cc, xx, :, 2 * k + m] = part[:, xx, cc].astype(BF)
-
-        loop(NB // 2, body, events)
 
     def pair_copy(g, r):
         return pltpu.make_async_remote_copy(
@@ -278,35 +310,38 @@
         orbital = sect * BN + lax.broadcasted_iota(jnp.int32, summed.shape, 1)
         out[8 * g : 8 * g + 8] = jnp.where(orbital < n2, summed, 0.0).astype(BF)
 
-    ACTIONS = dict(o=ag_own, n=ag_near, f=ag_far, e=ag_end, r1=red1, r2=red2, r3=red3, r4=red4, r5=red5, r6=red6, end=finish)
+    pieces, chunks = range(16), [(g, r) for g in range(GROUPS) for r in range(RC)]
+    o, n, f, e, h = ([functools.partial(act, p) for p in pieces] for act in (ag_own, ag_near, ag_far, ag_end, ag_half))
+    r1, r2, r3, r4, r5, r6 = (
+        {at: functools.partial(act, *at) for at in chunks} for act in (red1, red2, red3, red4, red5, red6)
+    )
 
     pl.semaphore_wait(barrier, len(friends))
 
-    def act(text):
-        words = text.split()
-        return [(w[:2], int(w[2]), int(w[3])) if w[0] == "r" else (w[0], int(w[1:])) for w in words]
-
-    run(act("o0 o1 o2 o3 o4"))
-    relay({7: act("o5 n0"), 9: act("n1"), 10: act("n2"), 12: act("n3")})
-    run(act("n4 n5 f0 o6 f1 o7 f2 f3 o8 f4 o9 f5 o10 o11 n6 n7 o12 e0 e1 e2 e3"))
-    turn(0)
-    run(act("o13"))
-    coulomb(0, {0: act("o14 n8 n9"), 2: act("n10 f6 n11 f7"), 3: act("n12"), 4: act("n13"), 5: act("o15 f8"), 6: act("f9 n14 f10")})
-    run(act("e4 e5 e6 e7"))
-    turn(1)
-    run(act("f11 f13"))
-    coulomb(1, {1: act("f12"), 2: act("f14"), 3: act("n15")})
-    run(act("e8 e9 e10 e11"))
-    ladder(0, 0, {0: act("f15")})
-    run(act("r100"))
-    ladder(0, 1, {})
-    run(act("r101 r200 e12 e13"))
-    early(1, {2: act("r201")})
-    run(act("e14 e15"))
-    ladder(1, 0, {})
-    run(act("r110 r300"))
-    ladder(1, 1, {})
-    run(act("r111 r301 r210 r211 r400 r401 r310 r311 r500 r501 r410 r411 r600 r601 r510 r511 r610 r611"))
+    run(o[0], o[1], o[2], o[3], o[4], o[5])
+    relay({7: (n[0], o[6], n[1],), 9: (n[2], o[7],), 10: (n[3],), 11: (n[4],)})
+    run(n[5], f[0], f[1], o[8], f[2], n[6], n[7], h[0], h[1], h[2], h[3])
+    turn_a()
+    run(f[3])
+    coulomb_a({0: (f[4], o[9],), 1: (o[10], f[5],), 2: (o[11],)})
+    run(o[12], f[6], f[7], n[8], e[0], e[1], e[2], e[3])
+    turn_b()
+    coulomb_b({0: (n[9], o[13], n[10],), 2: (o[14], n[11], n[12], f[8],)})
+    run(e[4], e[5], e[6], e[7])
+    turn_1()
+    run(o[15], f[9], f[10])
+    coulomb_1({0: (n[13],), 1: (f[11], f[12], n[14],), 2: (n[15], f[13],)})
+    run(e[8], e[9], e[10], e[11])
+    ladder(0, 0)
+    run(r1[0, 0], f[14])
+    ladder(0, 1)
+    run(r1[0, 1], f[15], r2[0, 0], e[12], e[13])
+    early()
+    run(r2[0, 1], e[14], e[15])
+    ladder(1, 0)
+    run(r1[1, 0], r3[0, 0])
+    ladder(1, 1)
+    run(r1[1, 1], r3[0, 1], r2[1, 0], r2[1, 1], r4[0, 0], r4[0, 1], r3[1, 0], r3[1, 1], r5[0, 0], r5[0, 1], r4[1, 0], r4[1, 1], r6[0, 0], r6[0, 1], r5[1, 0], r5[1, 1], r6[1, 0], r6[1, 1])
     finish(0)
     finish(1)
     for make in sent:
@@ -330,7 +365,9 @@
         out_specs=pl.BlockSpec(memory_space=vmem),
         scratch_shapes=[
             vmem((CB, QN, AN), BF),
-            vmem((CB * AN, QN), BF),
+            vmem((4 * AN, QN // 2), BF),
+            vmem((4 * AN, QN // 2), BF),
+            vmem((4 * AN, QN), BF),
             vmem((GROUPS, ROWS * SECTS, CB * DN), BF),
             vmem((QN, BN, DN), BF),
             vmem((BN, QN, DN), BF),
@@ -350,6 +387,7 @@
             vmem(whole + (2, NB) + spot, BF),
             vmem((GROUPS, RC * NB) + spot, F32),
             vmem((BN // 4, ROWS * SECTS, 4 * AN), F32),
+            vmem((BN, 4 * AN, DN), F32),
             dma((STAGES,)),
             dma((16, 7)),
             dma((16, SECTS)),

time: 67.3 us -> 64.2 us (0.954)
  Pallas kernels: 65.7 us -> 62.6 us
    pallas_call x1, Pallas kernels: 65.7 us -> 62.6 us  [per_device(): pl.pallas_call(kernel, out_shape=jax.ShapeDtypeStruct((GROUPS * 8, BN, AN...]
where the time goes in v3:
time: 64.2 us; the launch traced here: 64.1 us
  Pallas kernels  62.6 us (98%)
  local copies, waits for them, and re-layouts  1.47 us (2%)
    pallas_call x1, Pallas kernels, per_device(): pl.pallas_call(kernel, out_shape=jax.ShapeDtypeStruct((GROUPS * 8, BN, AN...  62.6 us
    unnamed x1, local copies, waits for them, and re-layouts  1.47 us

profile of v3, /device:TPU:2, one launch (start us, length us, event | category | flops | bytes accessed | tf_op | source)
XLA Modules:
  0.0 64.1 jit_solution(7496944066767026524)
XLA Ops:
  0.0 62.6 %shard_map.46 = bf16[16,16,128]{2,1,0:T(8,128)(2,1)} custom-call(s32[2]{0:T(128)} %counts.1, bf16[112,8,128]{2,1,0:T(8,128)(2,1)} %left.1, bf16[64,8,256]{2,1,0:T(8,128)(2,1)} %lam.1, bf16[896,16,256]{2,1,0:T(8,128)(2,1)} %right.1), custom_call_target="tpu_custom_call" | custom-call | flops 12000000000 | bytes 8000000 | tf_op jit(solution)/shard_map/pallas_call | solution.py:356
  62.6 1.5 %copy.6 = bf16[16,128,16]{1,2,0:T(8,128)(2,1)} copy(bf16[16,128,16]{1,2,0:T(8,128)(2,1)} %bitcast.1) | data formatting | bytes 131072

commit v4 on v3

--- a/solution.py
+++ b/solution.py
@@ -16,17 +16,18 @@
 BN = 16
 GROUPS, ROWS = 2, 32
 BLOCK = 4
-RC, NB = 2, 4
+CHUNKS = ((0, 0, 4), (0, 4, 4), (1, 0, 2), (1, 2, 2), (1, 4, 2), (1, 6, 2))
+Z_LEADS = (0, 0, 0, 1, 0, 0)
 STAGES = 14
 STEP = QN // STAGES
-Z_FIRST = (0, 0, 0, 1, 1, 1, 1, 0, 1, 0, 0, 1, 0, 1, 1, 1)
-FAR_PLUS = (0, 1, 0, 1, 1, 1, 0, 0, 1, 1, 0, 1, 0, 1, 1, 0)
+Z_FIRST = (0, 1, 0, 1, 0, 1, 1, 0, 1, 0, 1, 0, 1, 0, 1, 0)
+FAR_PLUS = (1, 1, 0, 0, 1, 1, 1, 1, 0, 0, 1, 0, 1, 0, 1, 0)
 
 
 def kernel(counts, left, lam, right, out,
            lbuf, ltra, ltrb, ltr, mbuf, rstage, rmat, coul, p32, pbf, rpair,
-           s32, sbf, xfar, xfwd, xdir, u32, ubf, zfar, zfwd, zdir,
-           v32, acc, acc0, rsem, ag_send, ag_recv, pr_send, pr_recv, x_send, x_recv, z_send, z_recv):
+           s32, sbf, xdir, u32, ubf, zdir,
+           v32, acc, acc0, lown, mown, in_sem, rsem, ag_send, ag_recv, hello, pr_send, pr_recv, x_send, x_recv, z_send, z_recv):
     sect, tile = lax.axis_index("sect"), lax.axis_index("tile")
     zl, y = sect // YN, sect % YN
     zh, x, core = tile // (2 * XN), (tile // 2) % XN, tile % 2
@@ -44,6 +45,7 @@
     zp, zm, zf = (zh + 1) % ZN, (zh + ZN - 1) % ZN, (zh + 2) % ZN
     at_xp, at_xm = tile_at(zh, xp, core), tile_at(zh, xm, core)
     at_zp, at_zm = tile_at(zp, x, core), tile_at(zm, x, core)
+    at_xf, at_zf = tile_at(zh, xf, core), tile_at(zf, x, core)
     at_pair = tile_at(zh, x, 1 - core)
 
     barrier = pltpu.get_barrier_semaphore()
@@ -55,11 +57,16 @@
         rows = pl.ds(k * STEP, STEP)
         return pltpu.make_async_copy(right.at[rows], rstage.at[rows], rsem.at[k])
 
+    pltpu.make_async_copy(left, lown, in_sem.at[0]).start()
+    pltpu.make_async_copy(lam, mown, in_sem.at[1]).start()
     for k in range(STAGES):
         stage_copy(k).start()
 
     n1, n2 = counts[0], counts[1]
-    own = pltpu.einshape("qca->cqa", left[...])
+    left_copy = pltpu.make_async_copy(left, lown, in_sem.at[0])
+    lam_copy = pltpu.make_async_copy(lam, mown, in_sem.at[1])
+    left_copy.wait()
+    own = pltpu.einshape("qca->cqa", lown[...])
     lane = lax.broadcasted_iota(jnp.int32, (QB, AN), 1)
     for c in range(CB):
         orbital = tile * CB + c
@@ -69,8 +76,9 @@
         lbuf[c, pl.ds(pl.multiple_of(sect * QB, 16), QB), :] = kept
     lane = lax.broadcasted_iota(jnp.int32, (ROWS, DN), 1)
     d_live = lane < jnp.where(lane < AN, n1, n2 + AN)
+    lam_copy.wait()
     for g in range(GROUPS):
-        mine = jnp.concatenate([lam[16 * u + 8 * g : 16 * u + 8 * g + 8] for u in range(4)], axis=0)
+        mine = jnp.concatenate([mown[16 * u + 8 * g : 16 * u + 8 * g + 8] for u in range(4)], axis=0)
         mine = pltpu.einshape("icd->cid", mine)
         for c in range(CB):
             kept = jnp.where(d_live, mine[c].astype(F32), 0.0).astype(BF)
@@ -222,126 +230,118 @@
         for quad in range(BN // 4):
             acc[quad] = product(1, quad, 0, CB // 2)
 
-    def ladder(g, r):
-        for k in range(NB // 2):
-            quad = r * (NB // 2) + k
+    def ladder(t):
+        g, first, count = CHUNKS[t]
+        for quad in range(first // 2, (first + count) // 2):
             block = product(g, quad, 0, CB) if g == 0 else acc[quad] + product(g, quad, CB // 2, CB)
             for m in range(2):
                 part = block[:, 2 * AN * m : 2 * AN * (m + 1)].reshape(ZN, XN, 2, 8, 2 * AN)
                 part = jnp.concatenate([part[..., :AN], part[..., AN:]], axis=3)
                 for cc in range(2):
                     for xx in range(XN):
-                        p32[g, r, cc, xx, :, 2 * k + m] = part[:, xx, cc]
-                        pbf[g, r, cc, xx, :, 2 * k + m] = part[:, xx, cc].astype(BF)
-
-    def pair_copy(g, r):
+                        p32[g, cc, xx, :, 2 * quad + m] = part[:, xx, cc]
+                        pbf[g, cc, xx, :, 2 * quad + m] = part[:, xx, cc].astype(BF)
+
+    def part_of(t):
+        g, first, count = CHUNKS[t]
+        return g, pl.ds(first, count)
+
+    def pair_copy(t):
+        g, js = part_of(t)
         return pltpu.make_async_remote_copy(
-            pbf.at[g, r, 1 - core], rpair.at[g, r], pr_send.at[g, r], pr_recv.at[g, r], at_pair, MESH)
-
-    def ring_copies(g, r, bf, far, fwd, direct, sends, recvs, cp, cm, cf, to_p, to_m):
-        half = bf.shape[3] // 2
-        lo, hi = pl.ds(0, half), pl.ds(half, half)
-        ends = (
-            (bf.at[g, r, cf, lo], far.at[g, r, 0], to_p),
-            (bf.at[g, r, cf, hi], far.at[g, r, 1], to_m),
-            (bf.at[g, r, cp, hi], direct.at[g, r, 0, hi], to_p),
-            (bf.at[g, r, cm, lo], direct.at[g, r, 1, lo], to_m),
-            (fwd.at[g, r, 0], direct.at[g, r, 0, lo], to_p),
-            (fwd.at[g, r, 1], direct.at[g, r, 1, hi], to_m),
-        )
-
-        def copy(k):
-            src, dst, where = ends[k]
-            return pltpu.make_async_remote_copy(src, dst, sends.at[g, r, k], recvs.at[g, r, k], where, MESH)
-
-        return copy
-
-    def x_copies(g, r):
-        return ring_copies(g, r, sbf, xfar, xfwd, xdir, x_send, x_recv, xp, xm, xf, at_xp, at_xm)
-
-    def z_copies(g, r):
-        return ring_copies(g, r, ubf, zfar, zfwd, zdir, z_send, z_recv, zp, zm, zf, at_zp, at_zm)
-
-    def ring_mid(g, r, ring, total, far, fwd, cp, cm):
-        half = total.shape[3] // 2
-        copies = ring(g, r)
-        copies(0).wait_recv()
-        fwd[g, r, 0] = (total[g, r, cp, :half] + far[g, r, 0].astype(F32)).astype(BF)
-        go(lambda: ring(g, r)(4))
-        copies(1).wait_recv()
-        fwd[g, r, 1] = (total[g, r, cm, half:] + far[g, r, 1].astype(F32)).astype(BF)
-        go(lambda: ring(g, r)(5))
-
-    def ring_end(g, r, copies, total, direct, me):
-        for k in range(2, 6):
-            copies(k).wait_recv()
-        return total[g, r, me] + direct[g, r, 0].astype(F32) + direct[g, r, 1].astype(F32)
-
-    def red1(g, r):
-        go(functools.partial(pair_copy, g, r))
-
-    def red2(g, r):
-        pair_copy(g, r).wait_recv()
+            pbf.at[g, 1 - core, :, :, js], rpair.at[g, :, :, js], pr_send.at[t], pr_recv.at[t], at_pair, MESH)
+
+    x_ends, z_ends = ((xf, at_xf), (xp, at_xp), (xm, at_xm)), ((zf, at_zf), (zp, at_zp), (zm, at_zm))
+
+    def first_copies(t, k):
+        g, js = part_of(t)
+        to, where = (z_ends if Z_LEADS[t] else x_ends)[k]
+        src = sbf.at[g, :, to, js] if Z_LEADS[t] else sbf.at[g, to, :, js]
+        return pltpu.make_async_remote_copy(src, xdir.at[g, k, :, js], x_send.at[t, k], x_recv.at[t, k], where, MESH)
+
+    def last_copies(t, k):
+        g, js = part_of(t)
+        to, where = (x_ends if Z_LEADS[t] else z_ends)[k]
+        return pltpu.make_async_remote_copy(
+            ubf.at[g, to, js], zdir.at[g, k, js], z_send.at[t, k], z_recv.at[t, k], where, MESH)
+
+    def red1(t):
+        go(functools.partial(pair_copy, t))
+
+    def red2(t):
+        g, js = part_of(t)
+        pair_copy(t).wait_recv()
         for xx in range(XN):
-            total = p32[g, r, core, xx] + rpair[g, r, xx].astype(F32)
-            s32[g, r, xx] = total
-            sbf[g, r, xx] = total.astype(BF)
-        for k in range(4):
-            go(functools.partial(lambda k: x_copies(g, r)(k), k))
-
-    def red3(g, r):
-        ring_mid(g, r, x_copies, s32, xfar, xfwd, xp, xm)
-
-    def red4(g, r):
-        total = ring_end(g, r, x_copies(g, r), s32, xdir, x)
-        u32[g, r] = total
-        ubf[g, r] = total.astype(BF)
-        for k in range(4):
-            go(functools.partial(lambda k: z_copies(g, r)(k), k))
-
-    def red5(g, r):
-        ring_mid(g, r, z_copies, u32, zfar, zfwd, zp, zm)
-
-    def red6(g, r):
-        v32[g, r * NB : (r + 1) * NB] = ring_end(g, r, z_copies(g, r), u32, zdir, zh)
+            total = p32[g, core, xx, :, js] + rpair[g, xx, :, js].astype(F32)
+            s32[g, xx, :, js] = total
+            sbf[g, xx, :, js] = total.astype(BF)
+        for k in range(3):
+            go(functools.partial(first_copies, t, k))
+
+    def red4(t):
+        g, js = part_of(t)
+        for k in range(3):
+            first_copies(t, k).wait_recv()
+        total = s32[g, :, zh, js] if Z_LEADS[t] else s32[g, x, :, js]
+        for k in range(3):
+            total = total + xdir[g, k, :, js].astype(F32)
+        u32[g, :, js] = total
+        ubf[g, :, js] = total.astype(BF)
+        for k in range(3):
+            go(functools.partial(last_copies, t, k))
+
+    def red6(t):
+        g, js = part_of(t)
+        for k in range(3):
+            last_copies(t, k).wait_recv()
+        total = u32[g, x if Z_LEADS[t] else zh, js]
+        for k in range(3):
+            total = total + zdir[g, k, js].astype(F32)
+        v32[g, js] = total
+
+    def greet():
+        pl.semaphore_wait(hello, 4)
 
     def finish(g):
         summed = pltpu.einshape("bia->iba", v32[g].reshape(BN, 8, AN))
         orbital = sect * BN + lax.broadcasted_iota(jnp.int32, summed.shape, 1)
         out[8 * g : 8 * g + 8] = jnp.where(orbital < n2, summed, 0.0).astype(BF)
 
-    pieces, chunks = range(16), [(g, r) for g in range(GROUPS) for r in range(RC)]
-    o, n, f, e, h = ([functools.partial(act, p) for p in pieces] for act in (ag_own, ag_near, ag_far, ag_end, ag_half))
-    r1, r2, r3, r4, r5, r6 = (
-        {at: functools.partial(act, *at) for at in chunks} for act in (red1, red2, red3, red4, red5, red6)
-    )
+    o, n, f, e, h = ([functools.partial(act, p) for p in range(16)] for act in (ag_own, ag_near, ag_far, ag_end, ag_half))
+    r1, r2, r4, r6 = ([functools.partial(act, t) for t in range(len(CHUNKS))] for act in (red1, red2, red4, red6))
 
     pl.semaphore_wait(barrier, len(friends))
+    for friend in (at_xp, at_xm, at_zp, at_zm):
+        pl.semaphore_signal(hello, inc=1, device_id=friend, device_id_type=MESH)
 
     run(o[0], o[1], o[2], o[3], o[4], o[5])
-    relay({7: (n[0], o[6], n[1],), 9: (n[2], o[7],), 10: (n[3],), 11: (n[4],)})
-    run(n[5], f[0], f[1], o[8], f[2], n[6], n[7], h[0], h[1], h[2], h[3])
+    relay({8: (o[6], n[0],), 9: (o[7], n[1], n[2],), 11: (n[3],), 12: (n[4],)})
+    run(n[5], n[6], f[0], n[7], o[8], f[1], f[2], o[9], h[0], h[1], h[2], h[3])
     turn_a()
-    run(f[3])
-    coulomb_a({0: (f[4], o[9],), 1: (o[10], f[5],), 2: (o[11],)})
-    run(o[12], f[6], f[7], n[8], e[0], e[1], e[2], e[3])
+    run(o[10], f[3])
+    coulomb_a({0: (f[4], o[11], f[5],), 1: (o[12], f[6],), 2: (o[13], f[7],)})
+    run(o[14], n[8], e[0], e[1], e[2], e[3])
     turn_b()
-    coulomb_b({0: (n[9], o[13], n[10],), 2: (o[14], n[11], n[12], f[8],)})
+    coulomb_b({0: (n[9], n[10],), 1: (n[11],), 2: (n[12],)})
     run(e[4], e[5], e[6], e[7])
     turn_1()
-    run(o[15], f[9], f[10])
-    coulomb_1({0: (n[13],), 1: (f[11], f[12], n[14],), 2: (n[15], f[13],)})
+    run(o[15], n[13], n[14], f[9])
+    coulomb_1({0: (f[8], f[10], f[11],), 1: (f[12],), 2: (f[13], n[15], f[14],)})
     run(e[8], e[9], e[10], e[11])
-    ladder(0, 0)
-    run(r1[0, 0], f[14])
-    ladder(0, 1)
-    run(r1[0, 1], f[15], r2[0, 0], e[12], e[13])
+    ladder(0)
+    run(r1[0])
+    ladder(1)
+    run(r1[1], f[15], greet, r2[0], e[12], e[13])
     early()
-    run(r2[0, 1], e[14], e[15])
-    ladder(1, 0)
-    run(r1[1, 0], r3[0, 0])
-    ladder(1, 1)
-    run(r1[1, 1], r3[0, 1], r2[1, 0], r2[1, 1], r4[0, 0], r4[0, 1], r3[1, 0], r3[1, 1], r5[0, 0], r5[0, 1], r4[1, 0], r4[1, 1], r6[0, 0], r6[0, 1], r5[1, 0], r5[1, 1], r6[1, 0], r6[1, 1])
+    run(r2[1], e[14], e[15])
+    ladder(2)
+    run(r1[2])
+    ladder(3)
+    run(r1[3])
+    ladder(4)
+    run(r1[4], r4[0], r2[2], r2[3])
+    ladder(5)
+    run(r1[5], r2[4], r4[1], r2[5], r4[2], r6[0], r4[4], r4[5], r4[3], r6[1], r6[2], r6[3], r6[4], r6[5])
     finish(0)
     finish(1)
     for make in sent:
@@ -349,8 +349,7 @@
 
 
 def per_device(irrep_counts, chol_left, chol_right, lam):
-    whole = (GROUPS, RC)
-    spot = (16, AN)
+    spot = (BN // 2, 16, AN)
     vmem = pltpu.VMEM
     dma = pltpu.SemaphoreType.DMA
     summed = pl.pallas_call(
@@ -358,8 +357,8 @@
         out_shape=jax.ShapeDtypeStruct((GROUPS * 8, BN, AN), BF),
         in_specs=[
             pl.BlockSpec(memory_space=pltpu.SMEM),
-            pl.BlockSpec(memory_space=vmem),
-            pl.BlockSpec(memory_space=vmem),
+            pl.BlockSpec(memory_space=pl.ANY),
+            pl.BlockSpec(memory_space=pl.ANY),
             pl.BlockSpec(memory_space=pl.ANY),
         ],
         out_specs=pl.BlockSpec(memory_space=vmem),
@@ -372,31 +371,31 @@
             vmem((QN, BN, DN), BF),
             vmem((BN, QN, DN), BF),
             vmem((BN, AN, CB * DN), BF),
-            vmem(whole + (2, XN, ZN, NB) + spot, F32),
-            vmem(whole + (2, XN, ZN, NB) + spot, BF),
-            vmem(whole + (XN, ZN, NB) + spot, BF),
-            vmem(whole + (XN, ZN, NB) + spot, F32),
-            vmem(whole + (XN, ZN, NB) + spot, BF),
-            vmem(whole + (2, ZN // 2, NB) + spot, BF),
-            vmem(whole + (2, ZN // 2, NB) + spot, BF),
-            vmem(whole + (2, ZN, NB) + spot, BF),
-            vmem(whole + (ZN, NB) + spot, F32),
-            vmem(whole + (ZN, NB) + spot, BF),
-            vmem(whole + (2, NB // 2) + spot, BF),
-            vmem(whole + (2, NB // 2) + spot, BF),
-            vmem(whole + (2, NB) + spot, BF),
-            vmem((GROUPS, RC * NB) + spot, F32),
+            vmem((GROUPS, 2, XN, ZN) + spot, F32),
+            vmem((GROUPS, 2, XN, ZN) + spot, BF),
+            vmem((GROUPS, XN, ZN) + spot, BF),
+            vmem((GROUPS, XN, ZN) + spot, F32),
+            vmem((GROUPS, XN, ZN) + spot, BF),
+            vmem((GROUPS, 3, ZN) + spot, BF),
+            vmem((GROUPS, ZN) + spot, F32),
+            vmem((GROUPS, ZN) + spot, BF),
+            vmem((GROUPS, 3) + spot, BF),
+            vmem((GROUPS,) + spot, F32),
             vmem((BN // 4, ROWS * SECTS, 4 * AN), F32),
             vmem((BN, 4 * AN, DN), F32),
+            vmem((QB, CB, AN), BF),
+            vmem((SECTS * 8, CB, DN), BF),
+            dma((2,)),
             dma((STAGES,)),
             dma((16, 7)),
             dma((16, SECTS)),
-            dma(whole),
-            dma(whole),
-            dma(whole + (6,)),
-            dma(whole + (6,)),
-            dma(whole + (6,)),
-            dma(whole + (6,)),
+            pltpu.SemaphoreType.REGULAR,
+            dma((len(CHUNKS),)),
+            dma((len(CHUNKS),)),
+            dma((len(CHUNKS), 3)),
+            dma((len(CHUNKS), 3)),
+            dma((len(CHUNKS), 3)),
+            dma((len(CHUNKS), 3)),
         ],
         compiler_params=pltpu.CompilerParams(
             collective_id=0, has_side_effects=True, vmem_limit_bytes=56 << 20

time: 64.2 us -> 63.1 us (0.983)
  Pallas kernels: 62.6 us -> 61 us
    pallas_call x1, Pallas kernels: 62.6 us -> 61 us  [per_device(): pl.pallas_call(kernel, out_shape=jax.ShapeDtypeStruct((GROUPS * 8, BN, AN...]
where the time goes in v4:
time: 63.1 us; the launch traced here: 62.5 us
  Pallas kernels  61 us (97%)
  local copies, waits for them, and re-layouts  1.47 us (2%)
    pallas_call x1, Pallas kernels, per_device(): pl.pallas_call(kernel, out_shape=jax.ShapeDtypeStruct((GROUPS * 8, BN, AN...  61 us
    unnamed x1, local copies, waits for them, and re-layouts  1.47 us

profile of v4, /device:TPU:2, one launch (start us, length us, event | category | flops | bytes accessed | tf_op | source)
XLA Modules:
  0.0 62.5 jit_solution(11108585720771801327)
XLA Ops:
  0.0 61.0 %shard_map.46 = bf16[16,16,128]{2,1,0:T(8,128)(2,1)} custom-call(s32[2]{0:T(128)} %counts.1, bf16[112,8,128]{2,1,0:T(8,128)(2,1)} %left.1, bf16[64,8,256]{2,1,0:T(8,128)(2,1)} %lam.1, bf16[896,16,256]{2,1,0:T(8,128)(2,1)} %right.1), custom_call_target="tpu_custom_call" | custom-call | flops 12000000000 | bytes 8000000 | tf_op jit(solution)/shard_map/pallas_call | solution.py:355
  61.0 1.5 %copy.6 = bf16[16,128,16]{1,2,0:T(8,128)(2,1)} copy(bf16[16,128,16]{1,2,0:T(8,128)(2,1)} %bitcast.1) | data formatting | bytes 131072

commit v5 on v4

--- a/solution.py
+++ b/solution.py
@@ -17,11 +17,11 @@
 GROUPS, ROWS = 2, 32
 BLOCK = 4
 CHUNKS = ((0, 0, 4), (0, 4, 4), (1, 0, 2), (1, 2, 2), (1, 4, 2), (1, 6, 2))
-Z_LEADS = (0, 0, 0, 1, 0, 0)
+Z_LEADS = (0, 1, 0, 0, 0, 0)
 STAGES = 14
 STEP = QN // STAGES
-Z_FIRST = (0, 1, 0, 1, 0, 1, 1, 0, 1, 0, 1, 0, 1, 0, 1, 0)
-FAR_PLUS = (1, 1, 0, 0, 1, 1, 1, 1, 0, 0, 1, 0, 1, 0, 1, 0)
+Z_FIRST = (1, 1, 0, 1, 0, 0, 0, 1, 1, 0, 0, 1, 1, 1, 0, 0)
+FAR_PLUS = (1, 1, 0, 0, 1, 1, 0, 0, 1, 1, 0, 0, 1, 1, 0, 1)
 
 
 def kernel(counts, left, lam, right, out,
@@ -308,41 +308,42 @@
         out[8 * g : 8 * g + 8] = jnp.where(orbital < n2, summed, 0.0).astype(BF)
 
     o, n, f, e, h = ([functools.partial(act, p) for p in range(16)] for act in (ag_own, ag_near, ag_far, ag_end, ag_half))
+    done = functools.partial(finish, 0)
     r1, r2, r4, r6 = ([functools.partial(act, t) for t in range(len(CHUNKS))] for act in (red1, red2, red4, red6))
 
     pl.semaphore_wait(barrier, len(friends))
     for friend in (at_xp, at_xm, at_zp, at_zm):
         pl.semaphore_signal(hello, inc=1, device_id=friend, device_id_type=MESH)
 
-    run(o[0], o[1], o[2], o[3], o[4], o[5])
-    relay({8: (o[6], n[0],), 9: (o[7], n[1], n[2],), 11: (n[3],), 12: (n[4],)})
-    run(n[5], n[6], f[0], n[7], o[8], f[1], f[2], o[9], h[0], h[1], h[2], h[3])
+    run(o[0], o[1], o[2], o[3], o[4], o[5], o[6], o[7])
+    relay({9: (n[0],), 11: (n[1],)})
+    run(n[2], n[3], n[4], n[5], n[6], n[7], f[0], o[8], f[1], f[2], o[9], h[0], h[1], h[2], h[3])
     turn_a()
     run(o[10], f[3])
-    coulomb_a({0: (f[4], o[11], f[5],), 1: (o[12], f[6],), 2: (o[13], f[7],)})
-    run(o[14], n[8], e[0], e[1], e[2], e[3])
+    coulomb_a({0: (f[4], f[6],), 1: (o[11], f[5], f[7],), 2: (o[12],)})
+    run(o[13], n[8], e[0], e[1], e[2], e[3])
     turn_b()
-    coulomb_b({0: (n[9], n[10],), 1: (n[11],), 2: (n[12],)})
-    run(e[4], e[5], e[6], e[7])
+    run(n[9], o[14])
+    coulomb_b({0: (n[10],), 1: (o[15], n[11],)})
+    run(n[12], f[8], e[4], e[5], e[6], e[7])
     turn_1()
-    run(o[15], n[13], n[14], f[9])
-    coulomb_1({0: (f[8], f[10], f[11],), 1: (f[12],), 2: (f[13], n[15], f[14],)})
-    run(e[8], e[9], e[10], e[11])
+    run(n[13])
+    coulomb_1({0: (f[9], f[10], n[14],), 1: (n[15], f[11],), 2: (f[12],)})
+    run(f[14], f[13], e[8], e[9], e[10], e[11])
     ladder(0)
-    run(r1[0])
+    run(r1[0], f[15])
     ladder(1)
-    run(r1[1], f[15], greet, r2[0], e[12], e[13])
+    run(r1[1], e[12], e[13])
     early()
-    run(r2[1], e[14], e[15])
+    run(greet, r2[0], r2[1], e[14], e[15])
     ladder(2)
     run(r1[2])
     ladder(3)
     run(r1[3])
     ladder(4)
-    run(r1[4], r4[0], r2[2], r2[3])
+    run(r1[4])
     ladder(5)
-    run(r1[5], r2[4], r4[1], r2[5], r4[2], r6[0], r4[4], r4[5], r4[3], r6[1], r6[2], r6[3], r6[4], r6[5])
-    finish(0)
+    run(r1[5], r2[2], r2[3], r2[4], r2[5], r4[0], r4[2], r4[3], r4[1], r4[4], r4[5], r6[0], r6[2], r6[1], done, r6[3], r6[4], r6[5])
     finish(1)
     for make in sent:
         make().wait_send()

time: 63.1 us -> 60.4 us (0.957)
  Pallas kernels: 61 us -> 58.1 us
    pallas_call x1, Pallas kernels: 61 us -> 58.1 us  [per_device(): pl.pallas_call(kernel, out_shape=jax.ShapeDtypeStruct((GROUPS * 8, BN, AN...]
where the time goes in v5:
time: 60.4 us; the launch traced here: 59.5 us
  Pallas kernels  58.1 us (96%)
  local copies, waits for them, and re-layouts  1.47 us (2%)
    pallas_call x1, Pallas kernels, per_device(): pl.pallas_call(kernel, out_shape=jax.ShapeDtypeStruct((GROUPS * 8, BN, AN...  58.1 us
    unnamed x1, local copies, waits for them, and re-layouts  1.47 us

profile of v5, /device:TPU:2, one launch (start us, length us, event | category | flops | bytes accessed | tf_op | source)
XLA Modules:
  0.0 59.5 jit_solution(12707647806343707532)
XLA Ops:
  0.0 58.1 %shard_map.46 = bf16[16,16,128]{2,1,0:T(8,128)(2,1)} custom-call(s32[2]{0:T(128)} %counts.1, bf16[112,8,128]{2,1,0:T(8,128)(2,1)} %left.1, bf16[64,8,256]{2,1,0:T(8,128)(2,1)} %lam.1, bf16[896,16,256]{2,1,0:T(8,128)(2,1)} %right.1), custom_call_target="tpu_custom_call" | custom-call | flops 12000000000 | bytes 8000000 | tf_op jit(solution)/shard_map/pallas_call | solution.py:356
  58.1 1.5 %copy.6 = bf16[16,128,16]{1,2,0:T(8,128)(2,1)} copy(bf16[16,128,16]{1,2,0:T(8,128)(2,1)} %bitcast.1) | data formatting | bytes 131072

commit v6 on v4

--- a/solution.py
+++ b/solution.py
@@ -20,8 +20,8 @@
 Z_LEADS = (0, 0, 0, 1, 0, 0)
 STAGES = 14
 STEP = QN // STAGES
-Z_FIRST = (0, 1, 0, 1, 0, 1, 1, 0, 1, 0, 1, 0, 1, 0, 1, 0)
-FAR_PLUS = (1, 1, 0, 0, 1, 1, 1, 1, 0, 0, 1, 0, 1, 0, 1, 0)
+Z_FIRST = (1, 1, 0, 1, 0, 0, 1, 0, 1, 0, 1, 0, 1, 1, 1, 0)
+FAR_PLUS = (1, 1, 0, 0, 1, 1, 0, 0, 1, 0, 0, 1, 1, 1, 1, 1)
 
 
 def kernel(counts, left, lam, right, out,
@@ -308,30 +308,30 @@
         out[8 * g : 8 * g + 8] = jnp.where(orbital < n2, summed, 0.0).astype(BF)
 
     o, n, f, e, h = ([functools.partial(act, p) for p in range(16)] for act in (ag_own, ag_near, ag_far, ag_end, ag_half))
+    done = functools.partial(finish, 0)
     r1, r2, r4, r6 = ([functools.partial(act, t) for t in range(len(CHUNKS))] for act in (red1, red2, red4, red6))
 
     pl.semaphore_wait(barrier, len(friends))
     for friend in (at_xp, at_xm, at_zp, at_zm):
         pl.semaphore_signal(hello, inc=1, device_id=friend, device_id_type=MESH)
 
-    run(o[0], o[1], o[2], o[3], o[4], o[5])
-    relay({8: (o[6], n[0],), 9: (o[7], n[1], n[2],), 11: (n[3],), 12: (n[4],)})
-    run(n[5], n[6], f[0], n[7], o[8], f[1], f[2], o[9], h[0], h[1], h[2], h[3])
+    run(o[0], o[1], o[2], o[3])
+    relay({2: (o[4],), 4: (o[5],), 6: (o[6],), 8: (o[7], n[0],), 10: (n[1],), 12: (n[2],)})
+    run(n[3], n[4], n[5], o[8], n[6], n[7], f[0], o[9], f[1], f[2], o[10], h[0], h[1], h[2], h[3])
     turn_a()
-    run(o[10], f[3])
-    coulomb_a({0: (f[4], o[11], f[5],), 1: (o[12], f[6],), 2: (o[13], f[7],)})
-    run(o[14], n[8], e[0], e[1], e[2], e[3])
+    run(f[3])
+    coulomb_a({0: (f[4], o[11],), 1: (f[5], n[8],), 2: (f[6], f[7], o[12],)})
+    run(n[9], o[13], e[0], e[1], e[2], e[3])
     turn_b()
-    coulomb_b({0: (n[9], n[10],), 1: (n[11],), 2: (n[12],)})
-    run(e[4], e[5], e[6], e[7])
+    coulomb_b({0: (n[10],), 1: (n[11], o[14],), 2: (f[8], o[15],)})
+    run(n[12], f[9], e[4], e[5], e[6], e[7])
     turn_1()
-    run(o[15], n[13], n[14], f[9])
-    coulomb_1({0: (f[8], f[10], f[11],), 1: (f[12],), 2: (f[13], n[15], f[14],)})
-    run(e[8], e[9], e[10], e[11])
+    coulomb_1({0: (f[10], n[13],), 1: (f[11],), 2: (n[14], n[15],)})
+    run(f[12], e[8], e[9], e[10], e[11])
     ladder(0)
-    run(r1[0])
+    run(r1[0], f[13])
     ladder(1)
-    run(r1[1], f[15], greet, r2[0], e[12], e[13])
+    run(r1[1], f[14], greet, r2[0], f[15], e[12], e[13])
     early()
     run(r2[1], e[14], e[15])
     ladder(2)
@@ -339,10 +339,9 @@
     ladder(3)
     run(r1[3])
     ladder(4)
-    run(r1[4], r4[0], r2[2], r2[3])
+    run(r1[4], r4[0], r2[2])
     ladder(5)
-    run(r1[5], r2[4], r4[1], r2[5], r4[2], r6[0], r4[4], r4[5], r4[3], r6[1], r6[2], r6[3], r6[4], r6[5])
-    finish(0)
+    run(r1[5], r2[3], r2[4], r4[1], r2[5], r4[2], r6[0], r4[4], r4[5], r4[3], r6[1], done, r6[2], r6[3], r6[4], r6[5])
     finish(1)
     for make in sent:
         make().wait_send()

time: 63.1 us -> 60.7 us (0.962)
  Pallas kernels: 61 us -> 58.9 us
    pallas_call x1, Pallas kernels: 61 us -> 58.9 us  [per_device(): pl.pallas_call(kernel, out_shape=jax.ShapeDtypeStruct((GROUPS * 8, BN, AN...]
where the time goes in v6:
time: 60.7 us; the launch traced here: 60.4 us
  Pallas kernels  58.9 us (97%)
  local copies, waits for them, and re-layouts  1.47 us (2%)
    pallas_call x1, Pallas kernels, per_device(): pl.pallas_call(kernel, out_shape=jax.ShapeDtypeStruct((GROUPS * 8, BN, AN...  58.9 us
    unnamed x1, local copies, waits for them, and re-layouts  1.47 us

profile of v6, /device:TPU:2, one launch (start us, length us, event | category | flops | bytes accessed | tf_op | source)
XLA Modules:
  0.0 60.4 jit_solution(13333209179318536418)
XLA Ops:
  0.0 58.9 %shard_map.46 = bf16[16,16,128]{2,1,0:T(8,128)(2,1)} custom-call(s32[2]{0:T(128)} %counts.1, bf16[112,8,128]{2,1,0:T(8,128)(2,1)} %left.1, bf16[64,8,256]{2,1,0:T(8,128)(2,1)} %lam.1, bf16[896,16,256]{2,1,0:T(8,128)(2,1)} %right.1), custom_call_target="tpu_custom_call" | custom-call | flops 12000000000 | bytes 8000000 | tf_op jit(solution)/shard_map/pallas_call | solution.py:354
  58.9 1.5 %copy.6 = bf16[16,128,16]{1,2,0:T(8,128)(2,1)} copy(bf16[16,128,16]{1,2,0:T(8,128)(2,1)} %bitcast.1) | data formatting | bytes 131072
